TPU v7x, 32 devices: a whole 2x2x4 slice. The times are simulated.
32 devices in a mesh: ctx: 8 (over z, x), head: 4 (over y, core).
Axes of the slice: x: 2, y: 2, z: 4, core: 2. Of those that a mesh axis runs over, the one named last changes fastest.
Arguments:
- queries: bfloat16 [3072, 8192], P('ctx', 'head'), may hold values from -160 to 160
- keys: bfloat16 [3072, 1024], P('ctx', 'head'), may hold values from -4 to 4
- values: bfloat16 [3072, 1024], P('ctx', 'head'), may hold values from -6 to 6
- keep_rows: int32 [8, 8, 8, 4], P('ctx', 'head'), may hold values from 0 to 383
- keep_dest: int32 [8, 8, 8], P('ctx', 'head'), may hold values from 0 to 7, as said below
- keep_count: int32 [8, 8, 8], P('ctx', 'head'), may hold values from 1 to 4, as said below
Outputs:
- attended: bfloat16 [3072, 8192], P('ctx', 'head')
- key_scores: float32 [3072], P('ctx')
- decode_cache: bfloat16 [8, 8, 4, 8, 256], P('ctx', None, None, 'head')
Inputs may be any that keep to these rules, and one draw needn't show every extreme that they name: For each source shard and head, keep_dest over j is a permutation of 0 to 7. `keep_count`: in every draw some decode shard receives 4 live slots in every block.
All inputs are finite; a program needn't handle non-finite values.
Results may differ from a plain program's by a relative error of at most 0.0045.
Values may be sent and summed in bfloat16 or wider, within the bound.
No kernel may reach another device: no remote copies, remote signals or barrier semaphores. Data moves between devices by JAX's collectives and lax.ppermute only.
A program may use at most 64 MiB of HBM per device.

v0:
```python
import jax
import jax.numpy as jnp
from jax import lax
from jax.sharding import PartitionSpec as P

HD = 128
KB = 4
QH = 64


def passed_along(block, axis, distance):
    devices = range(lax.axis_size(axis))
    route = [((i - distance) % len(devices), i) for i in devices]
    return lax.ppermute(block, axis, route)


def block_positions(shard, count, half):
    index = jnp.arange(2 * half, dtype=jnp.int32)
    return jnp.where(
        index < half, shard * half + index, (2 * count - 1 - shard) * half + index - half
    )


def on_device(queries, keys, values, keep_rows, keep_dest, keep_count):
    count = lax.axis_size("ctx")
    shard = lax.axis_index("ctx")
    tok = keys.shape[0]
    half = tok // 2
    groups = keys.shape[1] // HD
    scale = HD ** (-0.5)
    pair = jnp.concatenate([keys.reshape(tok, groups, HD), values.reshape(tok, groups, HD)], axis=2)
    block_index = jnp.arange(count, dtype=jnp.int32)
    slot = jnp.arange(KB, dtype=jnp.int32)
    outgoing = []
    for group in range(groups):
        rows_g = keep_rows[0, group]
        live_g = keep_count[0, group]
        dest_g = keep_dest[0, group]
        picked = jnp.take(pair[:, group], rows_g.reshape(-1), axis=0).reshape(count, KB, 2 * HD)
        picked = jnp.where(
            (slot[None, :] < live_g[:, None])[..., None], picked, jnp.zeros((), jnp.bfloat16)
        )
        match = dest_g[:, None] == block_index[None, :]
        inverse = jnp.sum(block_index[:, None] * match, axis=0)
        outgoing.append(jnp.take(picked, inverse, axis=0))
    outgoing = jnp.stack(outgoing, axis=2)[None]
    decode_cache = lax.all_to_all(outgoing, "ctx", split_axis=1, concat_axis=1, tiled=True)
    blocks = [pair]
    for step in range(2):
        blocks.append(passed_along(blocks[-1], "ctx", 1))
    kv_all = jnp.concatenate(blocks, 0)
    key_pos = jnp.concatenate(
        [block_positions((shard - step) % count, count, half) for step in range(3)]
    )
    query_pos = block_positions(shard, count, half)
    query_view = queries.reshape(tok, groups, -1, HD)
    column = jnp.zeros((3 * tok,), jnp.float32)
    results = []
    for group in range(groups):
        key_g = kv_all[:, group, :HD]
        val_g = kv_all[:, group, HD:]
        pieces = []
        for part_half in range(2):
            query_g = query_view[part_half * half : (part_half + 1) * half, group]
            score = (
                jnp.einsum("qrd,kd->rqk", query_g, key_g, preferred_element_type=jnp.float32)
                * scale
            )
            allowed = key_pos[None, :] <= query_pos[part_half * half : (part_half + 1) * half, None]
            score = jnp.where(allowed[None], score, -jnp.inf)
            top = jnp.max(score, -1, keepdims=True)
            weight = jnp.exp(score - top)
            total = jnp.sum(weight, -1, keepdims=True)
            product = jnp.einsum(
                "rqk,kd->qrd",
                weight.astype(jnp.bfloat16),
                val_g,
                preferred_element_type=jnp.float32,
            )
            pieces.append(product / jnp.transpose(total, (1, 0, 2)))
            column = column + jnp.sum(weight / total, axis=(0, 1))
        results.append(jnp.concatenate(pieces, 0))
    attended = jnp.stack(results, 1).reshape(tok, -1).astype(jnp.bfloat16)
    terms = column.reshape(3, tok) / QH
    carry = terms[2]
    for step in range(2):
        carry = passed_along(carry, "ctx", -1) + terms[1 - step]
    carry = lax.psum(carry, "head")
    return (attended, carry, decode_cache)


def solution(mesh):
    return jax.shard_map(
        on_device,
        mesh=mesh,
        in_specs=(
            P("ctx", "head"),
            P("ctx", "head"),
            P("ctx", "head"),
            P("ctx", "head", None, None),
            P("ctx", "head", None),
            P("ctx", "head", None),
        ),
        out_specs=(P("ctx", "head"), P("ctx"), P("ctx", None, None, "head", None)),
        check_vma=False,
    )
```

profile of v0, /device:TPU:0, one launch (start us, length us, event | category | flops | bytes accessed | tf_op | source)
XLA Modules:
  0.0 89.7 jit_solution(13728310644613227192)
XLA Ops:
  0.6 0.8 slice_bitcast_fusion.22
  1.5 0.7 fusion.76
  2.6 0.8 slice_bitcast_fusion.23
  3.4 1.1 %copy.58 = bf16[384,256]{0,1:T(8,128)(2,1)S(1)} copy(bf16[384,256]{1,0:T(8,128)(2,1)} %param.11) | data formatting | bytes 393216 | tf_op args[1]
  4.7 1.1 %copy.59 = bf16[384,256]{0,1:T(8,128)(2,1)S(1)} copy(bf16[384,256]{1,0:T(8,128)(2,1)} %param.12) | data formatting | bytes 393216 | tf_op args[2]
  6.0 0.6 gather_fusion
  9.1 0.6 copy.72
  9.7 7.3 %all-to-all-start = ((bf16[1,8,4,2,256]{4,3,2,0,1:T(2,128)(2,1)}), bf16[1,8,4,2,256]{4,3,2,0,1:T(2,128)(2,1)S(1)}, u32[]{:S(2)}, u32[]{:S(2)}) async-start(bf16[1,8,4,2,256]{4,3,2,0,1:T(2,128)(2,1)} %copy.72), calls=%async_computation | async-start | bytes 65536 | tf_op jit(solution)/shard_map/all_to_all | solution.py:47
  17.0 2.1 %collective-permute-start = (bf16[384,2,256]{2,0,1:T(8,128)(2,1)S(1)}, bf16[384,2,256]{2,0,1:T(8,128)(2,1)S(1)}, u32[]{:S(2)}, u32[]{:S(2)}) collective-permute-start(bf16[384,2,256]{2,0,1:T(8,128)(2,1)S(1)} %pad_maximum_fusion.2), channel_id=1, source_target_pairs={{28,0},{0,4},{4,8},{8,12},{12,16},{16,20},{20,24},{24,28},{29,1},{... | collective-permute-start | bytes 1179656 | tf_op jit(solution)/shard_map/ppermute | solution.py:14
  19.2 11.8 %collective-permute-done = bf16[384,2,256]{2,0,1:T(8,128)(2,1)S(1)} collective-permute-done((bf16[384,2,256]{2,0,1:T(8,128)(2,1)S(1)}, bf16[384,2,256]{2,0,1:T(8,128)(2,1)S(1)}, u32[]{:S(2)}, u32[]{:S(2)}) %collective-permute-start) | collective-permute-done | bytes 393248 | tf_op jit(solution)/shard_map/ppermute | solution.py:14
  31.3 1.9 %copy.62 = bf16[384,2048]{0,1:T(8,128)(2,1)S(1)} copy(bf16[384,2048]{1,0:T(8,128)(2,1)} %param.10) | data formatting | bytes 3145728 | tf_op args[0]
  33.2 10.1 %collective-permute-done.1 = bf16[384,2,256]{2,0,1:T(8,128)(2,1)S(1)} collective-permute-done((bf16[384,2,256]{2,0,1:T(8,128)(2,1)S(1)}, bf16[384,2,256]{2,0,1:T(8,128)(2,1)S(1)}, u32[]{:S(2)}, u32[]{:S(2)}) %collective-permute-start.1) | collective-permute-done | bytes 393248 | tf_op jit(solution)/shard_map/ppermute | solution.py:14
  43.4 1.9 %fusion.1 = (f32[8,192]{1,0:T(8,128)S(1)}, f32[1152,192,8]{0,1,2:T(8,128)S(1)}) fusion(pred[192,1152]{1,0:T(8,128)(4,1)S(1)} %get-tuple-element.24, bf16[384,2,8,128]{0,3,2,1:T(8,128)(2,1)S(1)} %bitcast.206, bf16[1152,2,256]{2,0,1:T(8,128)(2,1)S(1)} %pad_maximum_fusion.1), kind=kOutput, calls=%fused_computation.17 | convolution fusion | flops 458291712 | bytes 8124416 | tf_op jit(solution)/shard_map/qrd,kd->rqk/dot_general | solution.py:66
  45.3 1.9 %fusion.6 = f32[8,192]{1,0:T(8,128)S(1)} fusion(f32[1152,192,8]{0,1,2:T(8,128)S(1)} %get-tuple-element.34, f32[8,192]{1,0:T(8,128)S(1)} %get-tuple-element.33, pred[192,1152]{1,0:T(8,128)(4,1)S(1)} %get-tuple-element.24), kind=kLoop, calls=%fused_computation.22 | loop fusion | flops 7076352 | bytes 7311360 | tf_op jit(solution)/shard_map/reduce_sum | solution.py:73
  47.2 3.6 %divide_reduce_fusion.2 = (f32[1152]{0:T(1024)S(1)}, f32[8,192]{1,0:T(8,128)S(1)}, f32[1152,192,8]{0,1,2:T(8,128)S(1)}) fusion(f32[1152,192,8]{0,1,2:T(8,128)S(1)} %get-tuple-element.34, f32[8,192]{1,0:T(8,128)S(1)} %fusion.6, f32[8,192]{1,0:T(8,128)S(1)} %get-tuple-element.33, pred[192,1152]{1,0:T(8,128)(4,1)S(1)} %get-tuple-element.24, ...), kind=kOutput, calls=%fused_computation.14 | convolution fusion | flops 467137920 | bytes 15223296 | tf_op jit(solution)/shard_map/qrd,kd->rqk/dot_general | solution.py:66
  50.8 1.9 %fusion.51 = bf16[192,8,128]{2,0,1:T(8,128)(2,1)S(1)} fusion(f32[1152,192,8]{0,1,2:T(8,128)S(1)} %get-tuple-element.34, f32[8,192]{1,0:T(8,128)S(1)} %get-tuple-element.33, pred[192,1152]{1,0:T(8,128)(4,1)S(1)} %get-tuple-element.24, f32[192,8]{0,1:T(8,128)S(1)} %bitcast.218, bf16[1152,2,256]{2,0,1:T(8,128)(2,1)S(1)} %pad_maximum_fusion.1), kind=kOutput, calls=%fused_computation.47 | convolution fusion | flops 460455936 | bytes 8003584 | tf_op jit(solution)/shard_map/rqk,kd->qrd/dot_general | solution.py:74
  52.7 1.9 %fusion.10 = f32[8,192]{1,0:T(8,128)S(1)} fusion(f32[1152,192,8]{0,1,2:T(8,128)S(1)} %get-tuple-element.35, f32[8,192]{1,0:T(8,128)S(1)} %get-tuple-element.18, pred[192,1152]{1,0:T(8,128)(4,1)S(1)} %get-tuple-element.24), kind=kLoop, calls=%fused_computation.26 | loop fusion | flops 7076352 | bytes 7311360 | tf_op jit(solution)/shard_map/reduce_sum | solution.py:73
  54.6 1.8 %divide_reduce_fusion = f32[1152]{0:T(1024)S(1)} fusion(f32[1152,192,8]{0,1,2:T(8,128)S(1)} %get-tuple-element.35, f32[8,192]{1,0:T(8,128)S(1)} %fusion.10, f32[8,192]{1,0:T(8,128)S(1)} %get-tuple-element.18, pred[192,1152]{1,0:T(8,128)(4,1)S(1)} %get-tuple-element.24), kind=kLoop, calls=%fused_computation.12 | loop fusion | flops 8846208 | bytes 7315968 | tf_op jit(solution)/shard_map/reduce_sum | solution.py:81
  56.4 2.1 %fusion.39 = bf16[192,8,128]{2,0,1:T(8,128)(2,1)S(1)} fusion(f32[1152,192,8]{0,1,2:T(8,128)S(1)} %get-tuple-element.35, f32[8,192]{1,0:T(8,128)S(1)} %get-tuple-element.18, pred[192,1152]{1,0:T(8,128)(4,1)S(1)} %get-tuple-element.24, f32[192,8]{0,1:T(8,128)S(1)} %bitcast.216, bf16[1152,2,256]{2,0,1:T(8,128)(2,1)S(1)} %pad_maximum_fusion.1), kind=kOutput, calls=%fused_computation.43 | convolution fusion | flops 460455936 | bytes 8003584 | tf_op jit(solution)/shard_map/rqk,kd->qrd/dot_general | solution.py:74
  58.5 1.7 %fusion = (f32[8,192]{1,0:T(8,128)S(1)}, f32[1152,192,8]{0,1,2:T(8,128)S(1)}) fusion(pred[192,1152]{1,0:T(8,128)(4,1)S(1)} %get-tuple-element.23, bf16[384,2,8,128]{0,3,2,1:T(8,128)(2,1)S(1)} %bitcast.208, bf16[1152,2,256]{2,0,1:T(8,128)(2,1)S(1)} %pad_maximum_fusion.1), kind=kOutput, calls=%fused_computation.16 | convolution fusion | flops 458291712 | bytes 8124416 | tf_op jit(solution)/shard_map/qrd,kd->rqk/dot_general | solution.py:66
  60.2 1.9 %fusion.4 = f32[8,192]{1,0:T(8,128)S(1)} fusion(f32[1152,192,8]{0,1,2:T(8,128)S(1)} %get-tuple-element.37, f32[8,192]{1,0:T(8,128)S(1)} %get-tuple-element.36, pred[192,1152]{1,0:T(8,128)(4,1)S(1)} %get-tuple-element.23), kind=kLoop, calls=%fused_computation.20 | loop fusion | flops 7076352 | bytes 7311360 | tf_op jit(solution)/shard_map/reduce_sum | solution.py:73
  62.1 3.4 %divide_reduce_fusion.3 = (f32[1152]{0:T(1024)S(1)}, f32[8,192]{1,0:T(8,128)S(1)}, f32[1152,192,8]{0,1,2:T(8,128)S(1)}) fusion(f32[1152,192,8]{0,1,2:T(8,128)S(1)} %get-tuple-element.37, f32[8,192]{1,0:T(8,128)S(1)} %fusion.4, f32[8,192]{1,0:T(8,128)S(1)} %get-tuple-element.36, pred[192,1152]{1,0:T(8,128)(4,1)S(1)} %get-tuple-element.23, ...), kind=kOutput, calls=%fused_computation.15 | convolution fusion | flops 467137920 | bytes 15223296 | tf_op jit(solution)/shard_map/qrd,kd->rqk/dot_general | solution.py:66
  65.5 1.9 %fusion.57 = bf16[192,8,128]{2,0,1:T(8,128)(2,1)S(1)} fusion(f32[1152,192,8]{0,1,2:T(8,128)S(1)} %get-tuple-element.37, f32[8,192]{1,0:T(8,128)S(1)} %get-tuple-element.36, pred[192,1152]{1,0:T(8,128)(4,1)S(1)} %get-tuple-element.23, f32[192,8]{0,1:T(8,128)S(1)} %bitcast.217, bf16[1152,2,256]{2,0,1:T(8,128)(2,1)S(1)} %pad_maximum_fusion.1), kind=kOutput, calls=%fused_computation.49 | convolution fusion | flops 460455936 | bytes 8003584 | tf_op jit(solution)/shard_map/rqk,kd->qrd/dot_general | solution.py:74
  67.4 1.9 %fusion.8 = f32[8,192]{1,0:T(8,128)S(1)} fusion(f32[1152,192,8]{0,1,2:T(8,128)S(1)} %get-tuple-element.38, f32[8,192]{1,0:T(8,128)S(1)} %get-tuple-element.20, pred[192,1152]{1,0:T(8,128)(4,1)S(1)} %get-tuple-element.23), kind=kLoop, calls=%fused_computation.24 | loop fusion | flops 7076352 | bytes 7311360 | tf_op jit(solution)/shard_map/reduce_sum | solution.py:73
  69.3 1.8 %divide_reduce_fusion.1 = f32[1152]{0:T(1024)S(1)} fusion(f32[1152,192,8]{0,1,2:T(8,128)S(1)} %get-tuple-element.38, f32[8,192]{1,0:T(8,128)S(1)} %fusion.8, f32[8,192]{1,0:T(8,128)S(1)} %get-tuple-element.20, pred[192,1152]{1,0:T(8,128)(4,1)S(1)} %get-tuple-element.23), kind=kLoop, calls=%fused_computation.13 | loop fusion | flops 8846208 | bytes 7315968 | tf_op jit(solution)/shard_map/reduce_sum | solution.py:81
  71.1 1.9 %fusion.45 = bf16[192,8,128]{2,0,1:T(8,128)(2,1)S(1)} fusion(f32[1152,192,8]{0,1,2:T(8,128)S(1)} %get-tuple-element.38, f32[8,192]{1,0:T(8,128)S(1)} %get-tuple-element.20, pred[192,1152]{1,0:T(8,128)(4,1)S(1)} %get-tuple-element.23, f32[192,8]{0,1:T(8,128)S(1)} %bitcast.215, bf16[1152,2,256]{2,0,1:T(8,128)(2,1)S(1)} %pad_maximum_fusion.1), kind=kOutput, calls=%fused_computation.45 | convolution fusion | flops 460455936 | bytes 8003584 | tf_op jit(solution)/shard_map/rqk,kd->qrd/dot_general | solution.py:74
  73.3 3.4 %collective-permute-done.2 = f32[384]{0:T(512)S(1)} collective-permute-done((f32[384]{0:T(512)S(1)}, f32[384]{0:T(512)S(1)}, u32[]{:S(2)}, u32[]{:S(2)}) %collective-permute-start.2) | collective-permute-done | bytes 1568 | tf_op jit(solution)/shard_map/ppermute | solution.py:14
  76.7 2.7 %collective-permute-start.3 = (f32[384]{0:T(512)S(1)}, f32[384]{0:T(512)S(1)}, u32[]{:S(2)}, u32[]{:S(2)}) collective-permute-start(f32[384]{0:T(512)S(1)} %slice_add_fusion.1), channel_id=1, source_target_pairs={{4,0},{8,4},{12,8},{16,12},{20,16},{24,20},{28,24},{0,28},{5,1},{9... | collective-permute-start | bytes 4616 | tf_op jit(solution)/shard_map/ppermute | solution.py:14
  79.6 0.9 copy.67
  80.4 1.6 %copy.73 = bf16[384,2048]{1,0:T(8,128)(2,1)} copy(bf16[384,2048]{0,1:T(8,128)(2,1)S(1)} %bitcast.205) | data formatting | bytes 3145728
  82.1 6.2 %psum.7 = f32[384]{0:T(512)} all-reduce(f32[384]{0:T(512)S(1)} %slice_add_fusion), channel_id=1, replica_groups=mesh['ctx'=8,'head'=4] {'head'}, use_global_device_ids=true, to_apply=%region_12.13 | all-reduce | flops 384 | bytes 3072 | tf_op jit(solution)/shard_map/psum | solution.py:88
  88.3 1.4 %copy.84 = bf16[1,8,4,2,256]{4,3,2,1,0:T(2,128)(2,1)} copy(bf16[1,8,4,2,256]{4,3,2,1,0:T(2,128)(2,1)} %bitcast.212) | data formatting | bytes 65536
  (56 shorter events, 4.2 us)
Async XLA Ops:
  9.7 23.5 %all-to-all-start = ((bf16[1,8,4,2,256]{4,3,2,0,1:T(2,128)(2,1)}), bf16[1,8,4,2,256]{4,3,2,0,1:T(2,128)(2,1)S(1)}, u32[]{:S(2)}, u32[]{:S(2)}) async-start(bf16[1,8,4,2,256]{4,3,2,0,1:T(2,128)(2,1)} %copy.72), calls=%async_computation | async-start | bytes 65536 | tf_op jit(solution)/shard_map/all_to_all | solution.py:47
  17.0 14.0 %collective-permute-start = (bf16[384,2,256]{2,0,1:T(8,128)(2,1)S(1)}, bf16[384,2,256]{2,0,1:T(8,128)(2,1)S(1)}, u32[]{:S(2)}, u32[]{:S(2)}) collective-permute-start(bf16[384,2,256]{2,0,1:T(8,128)(2,1)S(1)} %pad_maximum_fusion.2), channel_id=1, source_target_pairs={{28,0},{0,4},{4,8},{8,12},{12,16},{16,20},{20,24},{24,28},{29,1},{... | collective-permute-start | bytes 1179656 | tf_op jit(solution)/shard_map/ppermute | solution.py:14
  31.0 12.4 %collective-permute-start.1 = (bf16[384,2,256]{2,0,1:T(8,128)(2,1)S(1)}, bf16[384,2,256]{2,0,1:T(8,128)(2,1)S(1)}, u32[]{:S(2)}, u32[]{:S(2)}) collective-permute-start(bf16[384,2,256]{2,0,1:T(8,128)(2,1)S(1)} %collective-permute-done), channel_id=1, source_target_pairs={{28,0},{0,4},{4,8},{8,12},{12,16},{16,20},{20,24},{24,28},{29,1},{... | collective-permute-start | bytes 1179656 | tf_op jit(solution)/shard_map/ppermute | solution.py:14
  33.2 14.0 %copy-start = (bf16[1,8,4,2,256]{4,3,2,0,1:T(2,128)(2,1)}, bf16[1,8,4,2,256]{4,3,2,0,1:T(2,128)(2,1)S(1)}, u32[]{:S(2)}) copy-start(bf16[1,8,4,2,256]{4,3,2,0,1:T(2,128)(2,1)S(1)} %all-to-all-done) | copy-start | bytes 98308
  73.1 3.6 %collective-permute-start.2 = (f32[384]{0:T(512)S(1)}, f32[384]{0:T(512)S(1)}, u32[]{:S(2)}, u32[]{:S(2)}) collective-permute-start(f32[384]{0:T(512)S(1)} %slice.105), channel_id=1, source_target_pairs={{4,0},{8,4},{12,8},{16,12},{20,16},{24,20},{28,24},{0,28},{5,1},{9... | collective-permute-start | bytes 4616 | tf_op jit(solution)/shard_map/ppermute | solution.py:14
  76.7 5.4 %collective-permute-start.3 = (f32[384]{0:T(512)S(1)}, f32[384]{0:T(512)S(1)}, u32[]{:S(2)}, u32[]{:S(2)}) collective-permute-start(f32[384]{0:T(512)S(1)} %slice_add_fusion.1), channel_id=1, source_target_pairs={{4,0},{8,4},{12,8},{16,12},{20,16},{24,20},{28,24},{0,28},{5,1},{9... | collective-permute-start | bytes 4616 | tf_op jit(solution)/shard_map/ppermute | solution.py:14
where the time goes:
time: 90.1 us; the launch traced here: 89.7 us
  waiting for transfers between devices  25.4 us (28%)
  matrix products  18.3 us (20%)
  local copies, waits for them, and re-layouts  14 us (16%)
  other arithmetic  12.8 us (14%)
  starting transfers between devices  12.1 us (13%)
  blocking collectives  6.22 us (7%)
  between operations  0.98 us (1%)
    ppermute x4, waiting for transfers between devices, passed_along(): return lax.ppermute(block, axis, route)  25.4 us
    dot_general x4, matrix products, on_device(): jnp.einsum('qrd,kd->rqk', query_g, key_g, preferred_element_type=jnp.floa...  10.6 us
    dot_general x4, matrix products, on_device(): jnp.einsum('rqk,kd->qrd', weight.astype(jnp.bfloat16), val_g, preferred_e...  7.72 us
    reduce_sum x4, other arithmetic, on_device(): total = jnp.sum(weight, -1, keepdims=True)  7.56 us
    all_to_all x1, starting transfers between devices, on_device(): lax.all_to_all(outgoing, 'ctx', split_axis=1, concat_axis=1, tiled=True)  7.25 us
    unnamed x7, local copies, waits for them, and re-layouts  7.08 us
    psum x1, blocking collectives, on_device(): carry = lax.psum(carry, 'head')  6.22 us
    ppermute x4, starting transfers between devices, passed_along(): return lax.ppermute(block, axis, route)  4.84 us
  transfers between devices with their start and end apart: 5, of which 3 were waited for; matrix products, arithmetic and copies ran while one was open for 6% of the time, Pallas kernels for 0%

commit v1 on v0

v1 whole, which is shorter than its diff:
```python
import functools
import math

import jax
import jax.numpy as jnp
from jax import lax
from jax.experimental import pallas as pl
from jax.experimental.pallas import tpu as pltpu
from jax.sharding import PartitionSpec as P

HD = 128
KB = 4
QH = 64
LANES = 128
CHUNK = 32
STEP_HEADS = 4
EXP2_SCALE = HD ** (-0.5) * math.log2(math.e)
VMEM = pl.BlockSpec(memory_space=pltpu.VMEM)
HBM = pl.BlockSpec(memory_space=pltpu.HBM)
MIB = 1024 * 1024


def tiles(width):
    return pl.cdiv(width, LANES) * LANES


def wide(column):
    return jnp.broadcast_to(column, (CHUNK, LANES))


def folded(block):
    return jnp.sum(block.reshape(-1, 8, LANES), axis=0)


def pick_rows(groups, k_ref, v_ref, rows_ref, dest_ref, live_ref, kept_ref, sent_ref, onehot):
    tok = k_ref.shape[0]
    me = lax.axis_index("ctx")
    count = dest_ref.shape[2]
    bits = count.bit_length() - 2
    size = kept_ref.shape[0]
    lanes = lax.broadcasted_iota(jnp.int32, (1, tok), 1)
    onehot[...] = jnp.zeros_like(onehot)
    for group in range(groups):
        @pl.loop(0, count, unroll=4)
        def _(j):
            dest = dest_ref[0, group, j]
            place = (dest + me) % 2
            for bit in range(bits):
                place = 2 * place + (dest >> (bit + 1)) % 2
            for slot in range(KB):
                row = jnp.where(slot < live_ref[0, group, j], rows_ref[0, group, slot, j], -1)
                at = (place * KB + slot) * groups + group
                onehot[group, pl.ds(at, 1)] = (lanes == row).astype(jnp.float32)
    for first, picked_ref in ((0, kept_ref), (size, sent_ref)):
        for ref, lane in ((k_ref, 0), (v_ref, HD)):
            picked_ref[:, lane : lane + HD] = sum(
                jnp.dot(
                    onehot[group, first : first + size].astype(jnp.bfloat16),
                    ref[:, group * HD : (group + 1) * HD],
                    preferred_element_type=jnp.float32,
                )
                for group in range(groups)
            ).astype(jnp.bfloat16)


def keep_kernel(groups, k_ref, v_ref, rows_hbm, dest_hbm, live_hbm, kept_ref, again1_ref, again2_ref, *refs):
    tok = k_ref.shape[0]
    *bit_refs, rows_ref, dest_ref, live_ref, onehot, sems = refs
    me = lax.axis_index("ctx")
    for bit, bit_ref in enumerate(bit_refs):
        bit_ref[...] = jnp.broadcast_to((me >> bit) % 2, bit_ref.shape)
    copies = [
        pltpu.make_async_copy(src, dst, sems.at[i])
        for i, (src, dst) in enumerate(
            ((rows_hbm, rows_ref), (dest_hbm, dest_ref), (live_hbm, live_ref))
        )
    ]
    for copy in copies:
        copy.start()
    again1_ref[:tok] = v_ref[...]
    again2_ref[...] = v_ref[...]
    for copy in copies:
        copy.wait()
    pick_rows(groups, k_ref, v_ref, rows_ref, dest_ref, live_ref, kept_ref, again1_ref.at[tok:], onehot)


def by_wraps(body):
    shard = lax.axis_index("ctx")
    for wraps in range(3):
        pl.when((shard == 2 - wraps) if wraps else (shard >= 2))(functools.partial(body, wraps))


def spans_of(wraps, half):
    if wraps == 0:
        return [(0, 2 * half, 4 * half)]
    return [(0, half, (3 - wraps) * half), (half, 2 * half, (4 + wraps) * half)]


def score_kernel(groups, qpk, half, q_ref, k_ref, k2_ref, k1_ref,
                 w_ref, inv_ref, own_ref, back1_ref, back2_ref, xkt, bias, s_buf, col):
    tok = 2 * half
    steps = qpk // STEP_HEADS
    edge = tiles(half)
    late_lo = 3 * half // LANES * LANES
    late_at = 3 * half - late_lo
    col[...] = jnp.zeros_like(col)
    row = lax.broadcasted_iota(jnp.int32, (half, edge), 0)
    column = lax.broadcasted_iota(jnp.int32, (half, edge), 1)
    masks = ((column >= half) | (column <= row), column <= row, column - late_at <= row)
    for i, mask in enumerate(masks):
        bias[i] = jnp.where(mask, 0.0, -jnp.inf)
    cut = jnp.where(lax.broadcasted_iota(jnp.int32, (CHUNK, LANES), 1) < half % LANES, 0.0, -jnp.inf)
    for group in range(groups):
        at = slice(group * HD, (group + 1) * HD)
        xkt[group] = jnp.concatenate(
            [k_ref[:half, at], k1_ref[:half, at], k2_ref[:half, at],
             k_ref[half:, at], k2_ref[half:, at], k1_ref[half:, at]], 0
        ).T

    def attend(wraps, group, step):
        spans = spans_of(wraps, half)

        def scores(i):
            at = pl.ds(pl.multiple_of(((group * steps + step) * STEP_HEADS + i) * HD, HD), HD)
            for first, last, keys in spans:
                s_buf[i, first:last, : tiles(keys)] = jnp.dot(
                    q_ref[first:last, at], xkt[group, :, : tiles(keys)],
                    preferred_element_type=jnp.float32,
                )

        def weights(i):
            head = (group * steps + step) * STEP_HEADS + i
            totals = {}
            for first, last, keys in spans:
                for r in range(first, last, CHUNK):
                    rows = slice(r, r + CHUNK)
                    early = r < half
                    inside = slice(r, r + CHUNK) if early else slice(r - half, r - half + CHUNK)
                    if early:
                        valid = (3 - wraps) * half
                    elif wraps == 0 and inside.stop + 3 * half <= late_lo + LANES:
                        valid = late_lo + LANES
                    else:
                        valid = (4 + wraps) * half
                    parts = []
                    for at in range(0, valid, LANES):
                        part = s_buf[i, rows, at : at + LANES]
                        if early and at < edge:
                            part += bias[1 if wraps == 2 else 0, inside, at : at + LANES]
                        elif not early and late_lo <= at < late_lo + edge:
                            part += bias[2, inside, at - late_lo : at - late_lo + LANES]
                        elif at + LANES > valid:
                            part += cut
                        parts.append(part)
                    peak = wide(jnp.max(functools.reduce(jnp.maximum, parts), axis=1, keepdims=True))
                    parts = [jnp.exp2((part - peak) * EXP2_SCALE) for part in parts]
                    inverse = 1.0 / wide(
                        jnp.sum(functools.reduce(jnp.add, parts), axis=1, keepdims=True)
                    )
                    inv_ref[head, rows] = inverse
                    for j, part in enumerate(parts):
                        w_ref[head, rows, j * LANES : (j + 1) * LANES] = part.astype(jnp.bfloat16)
                        part = folded(part * inverse)
                        totals[j] = totals[j] + part if j in totals else part
                    if len(parts) * LANES < tiles(keys):
                        w_ref[head, rows, len(parts) * LANES : tiles(keys)] = jnp.zeros(
                            (CHUNK, tiles(keys) - len(parts) * LANES), jnp.bfloat16
                        )
            for j, block in totals.items():
                col[:, j * LANES : (j + 1) * LANES] += block

        scores(0)
        for i in range(STEP_HEADS):
            if i + 1 < STEP_HEADS:
                scores(i + 1)
            weights(i)

    @by_wraps
    def _(wraps):
        for group in range(groups):
            pl.loop(0, steps)(functools.partial(attend, wraps, group))

    total = jnp.sum(col[...], axis=0, keepdims=True) * (1.0 / QH)
    own_ref[:, :half] = total[:, :half]
    own_ref[:, half:] = total[:, 3 * half : 4 * half]
    back1_ref[:, :half] = total[:, half : 2 * half]
    back1_ref[:, half:] = total[:, 5 * half :]
    back2_ref[:, :half] = total[:, 2 * half : 3 * half]
    back2_ref[:, half:] = total[:, 4 * half : 5 * half]


def value_kernel(group, qpk, half, v_ref, v1_ref, v2_ref, w_ref, inv_ref, pass_ref, *refs):
    tok = 2 * half
    steps = qpk // STEP_HEADS
    out_hbm, again_ref, xv, out_buf, sems = refs[-5:]
    again_ref[...] = pass_ref[...]
    at = slice(group * HD, (group + 1) * HD)
    xv[...] = jnp.concatenate(
        [v_ref[:half, at], v1_ref[:half, at], v2_ref[:half, at],
         v_ref[half:, at], v2_ref[half:, at], v1_ref[half:tok, at]], 0
    )

    def sent(step):
        first = (group * steps + step) * STEP_HEADS * HD
        at = pl.ds(pl.multiple_of(first, HD), STEP_HEADS * HD)
        return pltpu.make_async_copy(out_buf.at[step], out_hbm.at[:, at], sems.at[step])

    def attend(wraps, step):
        for i in range(STEP_HEADS):
            lanes = slice(i * HD, (i + 1) * HD)
            head = (group * steps + step) * STEP_HEADS + i
            for first, last, keys in spans_of(wraps, half):
                product = jnp.dot(
                    w_ref[head, first:last, : tiles(keys)], xv[: tiles(keys)],
                    preferred_element_type=jnp.float32,
                )
                out_buf[step, first:last, lanes] = (product * inv_ref[head, first:last]).astype(
                    jnp.bfloat16
                )
        sent(step).start()

    @by_wraps
    def _(wraps):
        pl.loop(0, steps)(functools.partial(attend, wraps))

    @pl.loop(0, steps)
    def _(step):
        sent(step).wait()


def cost(pairs, heads, half):
    return pl.CostEstimate(
        flops=heads * pairs * half * half * HD * 12,
        bytes_accessed=heads * half * HD * 64,
        transcendentals=heads * pairs * half * half,
    )


def keep(keys, values, *kept):
    tok = keys.shape[0]
    groups = keys.shape[1] // HD
    count = kept[1].shape[2]
    rows = groups * count // 2 * KB
    shapes = [
        jax.ShapeDtypeStruct((rows, 2 * HD), values.dtype),
        jax.ShapeDtypeStruct((tok + rows, groups * HD), values.dtype),
        jax.ShapeDtypeStruct(values.shape, values.dtype),
    ]
    shapes += [jax.ShapeDtypeStruct((groups * KB, 2 * HD), jnp.int32)] * (count.bit_length() - 1)
    return pl.pallas_call(
        functools.partial(keep_kernel, groups),
        out_shape=shapes,
        in_specs=[VMEM] * 2 + [HBM] * 3,
        out_specs=[VMEM] * len(shapes),
        scratch_shapes=[pltpu.SMEM(a.shape, a.dtype) for a in kept]
        + [pltpu.VMEM((groups, 2 * rows, tok), jnp.float32), pltpu.SemaphoreType.DMA((3,))],
        compiler_params=pltpu.CompilerParams(vmem_limit_bytes=8 * MIB),
        cost_estimate=cost(2, 16, tok // 2),
        name="keep_rows",
    )(keys, values, *kept)


def window_scores(queries, keys, k2, k1):
    tok, width = queries.shape
    half = tok // 2
    groups = keys.shape[1] // HD
    heads = width // HD
    most = 6 * half
    return pl.pallas_call(
        functools.partial(score_kernel, groups, heads // groups, half),
        out_shape=(
            jax.ShapeDtypeStruct((heads, tok, most), jnp.bfloat16),
            jax.ShapeDtypeStruct((heads, tok, LANES), jnp.float32),
            jax.ShapeDtypeStruct((1, tok), jnp.float32),
            jax.ShapeDtypeStruct((1, tok), jnp.float32),
            jax.ShapeDtypeStruct((1, tok), jnp.float32),
        ),
        in_specs=[VMEM] * 4,
        out_specs=(VMEM,) * 5,
        scratch_shapes=[
            pltpu.VMEM((groups, HD, most), jnp.bfloat16),
            pltpu.VMEM((3, half, tiles(half)), jnp.float32),
            pltpu.VMEM((STEP_HEADS, tok, most), jnp.float32),
            pltpu.VMEM((8, most), jnp.float32),
        ],
        compiler_params=pltpu.CompilerParams(vmem_limit_bytes=20 * MIB),
        cost_estimate=cost(7, heads, half),
        name="window_scores",
    )(queries, keys, k2, k1)


def ride(back, kept, v1):
    tok = back.shape[1]
    rows, width = kept.shape
    size = rows // 2
    top = groups_of_eight(pl.cdiv(tok, width))

    def kernel(back_ref, kept_ref, v1_ref, out_ref, stay_ref):
        out_ref[:top] = jnp.zeros((top, width), jnp.float32)
        for i in range(pl.cdiv(tok, width)):
            part = back_ref[:, i * width : min((i + 1) * width, tok)]
            out_ref[i : i + 1, : part.shape[1]] = part
        mine = (lax.axis_index("ctx") >> 1) % 2 == 1
        for i, (low, high) in enumerate(
            ((kept_ref[:size], kept_ref[size:]), (v1_ref[tok : tok + size], v1_ref[tok + size :]))
        ):
            stay_ref[i * size : (i + 1) * size] = jnp.where(mine, high, low)
            out_ref[top + i * size : top + (i + 1) * size] = jnp.where(mine, low, high).astype(jnp.float32)

    return pl.pallas_call(
        kernel,
        out_shape=(
            jax.ShapeDtypeStruct((top + rows, width), jnp.float32),
            jax.ShapeDtypeStruct((rows, width), kept.dtype),
        ),
        in_specs=[VMEM] * 3,
        out_specs=(VMEM,) * 2,
        compiler_params=pltpu.CompilerParams(vmem_limit_bytes=4 * MIB),
        name="ride",
    )(back, kept, v1)


def groups_of_eight(rows):
    return (rows + 7) // 8 * 8


def window_values(group, values, v1, v2, weights, inverse, passed, *attended):
    heads, tok, most = weights.shape
    groups = values.shape[1] // HD
    steps = heads // groups // STEP_HEADS
    return pl.pallas_call(
        functools.partial(value_kernel, group, heads // groups, tok // 2),
        out_shape=(
            jax.ShapeDtypeStruct((tok, heads * HD), jnp.bfloat16),
            jax.ShapeDtypeStruct(passed.shape, passed.dtype),
        ),
        in_specs=[VMEM] * 6 + [HBM] * len(attended),
        out_specs=(HBM, VMEM),
        scratch_shapes=[
            pltpu.VMEM((most, HD), jnp.bfloat16),
            pltpu.VMEM((steps, tok, STEP_HEADS * HD), jnp.bfloat16),
            pltpu.SemaphoreType.DMA((steps,)),
        ],
        input_output_aliases={6: 0} if attended else {},
        compiler_params=pltpu.CompilerParams(vmem_limit_bytes=12 * MIB),
        cost_estimate=cost(3, heads // groups, tok // 2),
        name="window_values",
    )(values, v1, v2, weights, inverse, passed, *attended)


def on_device(queries, keys, values, keep_rows, keep_dest, keep_count):
    count = lax.axis_size("ctx")
    heads = lax.axis_size("head")
    groups = keys.shape[1] // HD

    def along(block, distance):
        return lax.ppermute(block, "ctx", [(i, (i + distance) % count) for i in range(count)])

    def swap(block, axis, bit):
        return lax.ppermute(block, axis, [(i, i ^ bit) for i in range(lax.axis_size(axis))])

    k2 = along(keys, 2)
    k1 = along(keys, 1)
    kept, again1, again2, *bits = keep(
        keys, values, jnp.swapaxes(keep_rows, 2, 3), keep_dest, keep_count
    )
    v1 = along(again1, 1)
    v2 = along(again2, 2)
    weights, inverse, own, back1, back2 = window_scores(queries, keys, k2, k1)
    tok = keys.shape[0]
    riding, stay = ride(back2, kept, v1)
    back1, riding = along(back1, -1), along(riding, -2)
    attended, own = window_values(0, values, v1, v2, weights, inverse, own)
    width = riding.shape[1]
    top = riding.shape[0] - stay.shape[0]
    back2 = jnp.concatenate([riding[i : i + 1] for i in range(pl.cdiv(tok, width))], 1)[:, :tok]
    scores = own + back1 + back2

    shape = (1, 1, 2, -1, groups * KB, width)
    blocks = jnp.concatenate(
        [stay.reshape(shape), riding[top:].astype(stay.dtype).reshape(shape)], axis=1
    )
    flags = [bit > 0 for bit in bits]
    bit = 1
    while 2 << bit <= count or 1 << bit <= heads:
        if 4 << bit <= count:
            low, high = jnp.split(blocks, 2, axis=3)
            mine = flags[bit + 1]
            stay, sent = jnp.where(mine, high, low), jnp.where(mine, low, high)
            found = swap(sent, "ctx", 2 << bit)
            blocks = jnp.concatenate([jnp.where(mine, found, stay), jnp.where(mine, stay, found)])
        if 1 << bit <= heads:
            other = swap(scores, "head", 1 << bit - 1)
            if 2 << bit > heads:
                for group in range(1, groups):
                    attended, scores = window_values(
                        group, values, v1, v2, weights, inverse, scores, attended
                    )
            scores = scores + other
        bit += 1

    def merged(even, odd):
        return jnp.stack([even, odd], axis=1).reshape((-1,) + even.shape[1:])

    blocks = blocks[:, :, :, 0]
    same, above = blocks[:, 0], blocks[:, 1]
    blocks = merged(
        jnp.where(flags[1], jnp.roll(above, 1, axis=0), same), jnp.where(flags[1], same, above)
    )
    near, carried = blocks[:, 0], blocks[:, 1]
    decode_cache = merged(
        jnp.where(flags[0], carried, near), jnp.where(flags[0], near, jnp.roll(carried, -1, axis=0))
    )
    decode_cache = decode_cache.reshape(1, count, KB, groups, width)
    return (attended, scores.reshape(-1), decode_cache)


def solution(mesh):
    return jax.shard_map(
        on_device,
        mesh=mesh,
        in_specs=(
            P("ctx", "head"),
            P("ctx", "head"),
            P("ctx", "head"),
            P("ctx", "head", None, None),
            P("ctx", "head", None),
            P("ctx", "head", None),
        ),
        out_specs=(P("ctx", "head"), P("ctx"), P("ctx", None, None, "head", None)),
        check_vma=False,
    )
```

time: 90.1 us -> 35.7 us (0.40)
  waiting for transfers between devices: 25.4 us -> 4.51 us
  matrix products: 18.3 us -> 0 us
  Pallas kernels: 0 us -> 13.3 us
  other arithmetic: 12.8 us -> 0.67 us
  local copies, waits for them, and re-layouts: 14 us -> 4.56 us
  blocking collectives: 6.22 us -> 0 us
    ppermute x4 -> x9, waiting for transfers between devices: 25.4 us -> 4.51 us  [the longest x6 3.93 us: along(): lax.ppermute(block, 'ctx', [(i, (i + distance) % count) for i in range(co...]
    dot_general x8 -> x0, matrix products: 18.3 us -> none  [the longest x4 10.6 us: on_device(): jnp.einsum('qrd,kd->rqk', query_g, key_g, preferred_element_type=jnp.floa...]
    pallas_call x0 -> x5, Pallas kernels: none -> 13.3 us  [the longest x1 7.15 us: window_scores(): pl.pallas_call(functools.partial(score_kernel, groups, heads // groups, h...]
    reduce_sum x7 -> x0, other arithmetic: 11.3 us -> none  [the longest x4 7.56 us: on_device(): total = jnp.sum(weight, -1, keepdims=True)]
    all_to_all x1 -> x0, starting transfers between devices: 7.25 us -> none  [on_device(): lax.all_to_all(outgoing, 'ctx', split_axis=1, concat_axis=1, tiled=True)]
    ppermute x4 -> x9, starting transfers between devices: 4.84 us -> 11.7 us  [the longest x6 9.56 us: along(): lax.ppermute(block, 'ctx', [(i, (i + distance) % count) for i in range(co...]
    psum x1 -> x0, blocking collectives: 6.22 us -> none  [on_device(): carry = lax.psum(carry, 'head')]
    unnamed x7 -> x16, local copies, waits for them, and re-layouts: 7.08 us -> 3.91 us
  transfers between devices with their start and end apart: 5 -> 9, of which waited for: 3 -> 3; matrix products, arithmetic and copies ran while one was open for 6% -> 2% of each run, Pallas kernels for 0% -> 37%
where the time goes in v1:
time: 35.7 us; the launch traced here: 35.5 us
  Pallas kernels  13.3 us (37%)
  starting transfers between devices  11.7 us (33%)
  local copies, waits for them, and re-layouts  4.56 us (13%)
  waiting for transfers between devices  4.51 us (13%)
  between operations  0.83 us (2%)
  other arithmetic  0.67 us (2%)
    ppermute x6, starting transfers between devices, along(): lax.ppermute(block, 'ctx', [(i, (i + distance) % count) for i in range(co...  9.56 us
    pallas_call x1, Pallas kernels, window_scores(): pl.pallas_call(functools.partial(score_kernel, groups, heads // groups, h...  7.15 us
    pallas_call x2, Pallas kernels, window_values(): pl.pallas_call(functools.partial(value_kernel, group, heads // groups, to...  4.76 us
    ppermute x6, waiting for transfers between devices, along(): lax.ppermute(block, 'ctx', [(i, (i + distance) % count) for i in range(co...  3.93 us
    unnamed x16, local copies, waits for them, and re-layouts  3.91 us
    ppermute x3, starting transfers between devices, swap(): lax.ppermute(block, axis, [(i, i ^ bit) for i in range(lax.axis_size(axis...  2.13 us
    pallas_call x1, Pallas kernels, keep(): pl.pallas_call(functools.partial(keep_kernel, groups), out_shape=shapes,...  1.35 us
  transfers between devices with their start and end apart: 9, of which 3 were waited for; matrix products, arithmetic and copies ran while one was open for 2% of the time, Pallas kernels for 37%

profile of v1, /device:TPU:0, one launch (start us, length us, event | category | flops | bytes accessed | tf_op | source)
XLA Modules:
  0.0 35.5 jit_solution(455643172227353264)
XLA Ops:
  0.6 3.1 %collective-permute-start.2 = (bf16[384,256]{1,0:T(8,128)(2,1)}, bf16[384,256]{1,0:T(8,128)(2,1)S(1)}, u32[]{:S(2)}, u32[]{:S(2)}) collective-permute-start(bf16[384,256]{1,0:T(8,128)(2,1)} %k_ref.3), channel_id=1, source_target_pairs={{0,8},{4,12},{8,16},{12,20},{16,24},{20,28},{24,0},{28,4},{1,9},{5... | collective-permute-start | bytes 589832 | tf_op jit(solution)/shard_map/ppermute | solution.py:357
  3.7 1.5 %collective-permute-start.3 = (bf16[384,256]{1,0:T(8,128)(2,1)}, bf16[384,256]{1,0:T(8,128)(2,1)S(1)}, u32[]{:S(2)}, u32[]{:S(2)}) collective-permute-start(bf16[384,256]{1,0:T(8,128)(2,1)} %k_ref.3), channel_id=1, source_target_pairs={{0,4},{4,8},{8,12},{12,16},{16,20},{20,24},{24,28},{28,0},{1,5},{5... | collective-permute-start | bytes 589832 | tf_op jit(solution)/shard_map/ppermute | solution.py:357
  5.2 0.9 %copy-done = bf16[384,256]{1,0:T(8,128)(2,1)S(1)} copy-done((bf16[384,256]{1,0:T(8,128)(2,1)S(1)}, bf16[384,256]{1,0:T(8,128)(2,1)}, u32[]{:S(2)}) %copy-start) | copy-done | bytes 196632
  6.1 0.9 %copy-done.3 = bf16[384,256]{1,0:T(8,128)(2,1)S(1)} copy-done((bf16[384,256]{1,0:T(8,128)(2,1)S(1)}, bf16[384,256]{1,0:T(8,128)(2,1)}, u32[]{:S(2)}) %copy-start.3) | copy-done | bytes 196632
  7.1 0.7 %copy-done.5 = s32[1,2,8,4]{2,3,1,0:T(4,128)S(1)} copy-done((s32[1,2,8,4]{2,3,1,0:T(4,128)S(1)}, s32[1,2,8,4]{2,3,1,0:T(4,128)}, u32[]{:S(2)}) %copy-start.5) | copy-done | bytes 280
  7.7 0.7 %copy-done.6 = s32[1,2,8]{2,1,0:T(2,128)S(1)} copy-done((s32[1,2,8]{2,1,0:T(2,128)S(1)}, s32[1,2,8]{2,1,0:T(2,128)}, u32[]{:S(2)}) %copy-start.6) | copy-done | bytes 88
  8.4 0.7 %copy-done.7 = s32[1,2,8]{2,1,0:T(2,128)S(1)} copy-done((s32[1,2,8]{2,1,0:T(2,128)S(1)}, s32[1,2,8]{2,1,0:T(2,128)}, u32[]{:S(2)}) %copy-start.7) | copy-done | bytes 88
  9.1 1.3 %keep_rows.1 = (bf16[32,256]{1,0:T(8,128)(2,1)S(1)}, bf16[416,256]{1,0:T(8,128)(2,1)S(1)}, bf16[384,256]{1,0:T(8,128)(2,1)S(1)}, s32[8,256]{1,0:T(8,128)S(1)}, s...) custom-call(bf16[384,256]{1,0:T(8,128)(2,1)S(1)} %copy-done.3, bf16[384,256]{1,0:T(8,128)(2,1)S(1)} %copy-done, ...), custom_call_target="tpu_custom_call" | custom-call | flops 1811939328 | bytes 25165824 | tf_op jit(solution)/shard_map/keep_rows/pallas_call | solution.py:250
  10.5 1.6 %collective-permute-start.1 = (bf16[384,256]{1,0:T(8,128)(2,1)S(1)}, bf16[384,256]{1,0:T(8,128)(2,1)S(1)}, u32[]{:S(2)}, u32[]{:S(2)}) collective-permute-start(bf16[384,256]{1,0:T(8,128)(2,1)S(1)} %get-tuple-element.21), channel_id=1, source_target_pairs={{0,8},{4,12},{8,16},{12,20},{16,24},{20,28},{24,0},{28,4},{1,9},{5... | collective-permute-start | bytes 589832 | tf_op jit(solution)/shard_map/ppermute | solution.py:357
  12.1 1.5 %collective-permute-start = (bf16[416,256]{1,0:T(8,128)(2,1)S(1)}, bf16[416,256]{1,0:T(8,128)(2,1)S(1)}, u32[]{:S(2)}, u32[]{:S(2)}) collective-permute-start(bf16[416,256]{1,0:T(8,128)(2,1)S(1)} %get-tuple-element.20), channel_id=1, source_target_pairs={{0,4},{4,8},{8,12},{12,16},{16,20},{20,24},{24,28},{28,0},{1,5},{5... | collective-permute-start | bytes 638984 | tf_op jit(solution)/shard_map/ppermute | solution.py:357
  13.7 0.0 copy-start.1
  13.7 0.0 collective-permute-done.2.k2_ref
  13.7 3.1 %collective-permute-done.3.k1_ref = bf16[384,256]{1,0:T(8,128)(2,1)S(1)} collective-permute-done((bf16[384,256]{1,0:T(8,128)(2,1)}, bf16[384,256]{1,0:T(8,128)(2,1)S(1)}, u32[]{:S(2)}, u32[]{:S(2)}) %collective-permute-start.3) | collective-permute-done | bytes 196640 | tf_op jit(solution)/shard_map/ppermute | solution.py:357
  16.7 0.0 copy-done.2
  16.7 7.1 %window_scores.1 = (bf16[16,384,1152]{2,1,0:T(8,128)(2,1)S(1)}, f32[16,384,128]{2,1,0:T(8,128)S(1)}, f32[1,384]{1,0:T(1,128)S(1)}, f32[1,384]{1,0:T(1,128)S(1)}, f32[1,384]{1,0:T(1,128)S(1)}) custom-call(bf16[384,2048]{1,0:T(8,128)(2,1)S(1)} %copy-done.2, bf16[384,256]{1,0:T(8,128)(2,1)S(1)} %copy-done.4, ...), custom_call_target="tpu_custom_call" | custom-call | flops 6341787648 | bytes 25165824 | tf_op jit(solution)/shard_map/window_scores/pallas_call | solution.py:269
  23.9 0.0 collective-permute-start.4
  23.9 0.9 %collective-permute-done.v1_ref = bf16[416,256]{1,0:T(8,128)(2,1)S(1)} collective-permute-done((bf16[416,256]{1,0:T(8,128)(2,1)S(1)}, bf16[416,256]{1,0:T(8,128)(2,1)S(1)}, u32[]{:S(2)}, u32[]{:S(2)}) %collective-permute-start) | collective-permute-done | bytes 213024 | tf_op jit(solution)/shard_map/ppermute | solution.py:357
  24.8 1.8 %collective-permute-start.5 = (f32[40,256]{1,0:T(8,128)S(1)}, f32[40,256]{1,0:T(8,128)S(1)}, u32[]{:S(2)}, u32[]{:S(2)}) collective-permute-start(f32[40,256]{1,0:T(8,128)S(1)} %get-tuple-element.29), channel_id=1, source_target_pairs={{0,24},{4,28},{8,0},{12,4},{16,8},{20,12},{24,16},{28,20},{1,25},{... | collective-permute-start | bytes 122888 | tf_op jit(solution)/shard_map/ppermute | solution.py:357
  26.6 0.0 collective-permute-done.1.v2_ref
  26.6 0.0 copy-done.1
  26.6 2.5 %window_values.2 = (bf16[384,2048]{1,0:T(8,128)(2,1)}, f32[1,384]{1,0:T(1,128)S(1)}) custom-call(bf16[384,256]{1,0:T(8,128)(2,1)S(1)} %copy-done.1, bf16[416,256]{1,0:T(8,128)(2,1)S(1)} %collective-permute-done.v1_ref, bf16[384,256]{1,0:T(8,128)(2,1)S(1)} %collective-permute-done.1.v2_ref, bf16[16,384,1152]{2,1,0:T(8,128)(2,1)S(1)} %get-tuple-element.22.w_ref, ...), custom_call_target="tpu_custom_call" | custom-call | flops 1358954496 | bytes 12582912 | tf_op jit(solution)/shard_map/window_values/pallas_call | solution.py:331
  29.1 0.0 collective-permute-done.5
  29.1 0.0 collective-permute-done.4
  29.1 0.1 collective-permute-start.6
  29.2 0.5 %collective-permute-start.8 = (bf16[1,2,2,1,8,256]{5,4,3,2,1,0:T(8,128)(2,1)S(1)}, bf16[1,2,2,1,8,256]{5,4,3,2,1,0:T(8,128)(2,1)S(1)}, u32[]{:S(2)}, u32[]{:S(2)}) collective-permute-start(bf16[1,2,2,1,8,256]{5,4,3,2,1,0:T(8,128)(2,1)S(1)} %broadcast_select_fusion.3), channel_id=1, source_target_pairs={{0,16},{4,20},{8,24},{12,28},{16,0},{20,4},{24,8},{28,12},{1,17},{... | collective-permute-start | bytes 49160 | tf_op jit(solution)/shard_map/ppermute | solution.py:360
  29.8 0.6 %collective-permute-done.6 = f32[1,384]{1,0:T(1,128)S(1)} collective-permute-done((f32[1,384]{1,0:T(1,128)S(1)}, f32[1,384]{1,0:T(1,128)S(1)}, u32[]{:S(2)}, u32[]{:S(2)}) %collective-permute-start.6) | collective-permute-done | bytes 1568 | tf_op jit(solution)/shard_map/ppermute | solution.py:360
  30.3 1.5 %collective-permute-start.7 = (f32[1,384]{1,0:T(1,128)S(1)}, f32[1,384]{1,0:T(1,128)S(1)}, u32[]{:S(2)}, u32[]{:S(2)}) collective-permute-start(f32[1,384]{1,0:T(1,128)S(1)} %add.14.pass_ref), channel_id=1, source_target_pairs={{0,2},{1,3},{2,0},{3,1},{4,6},{5,7},{6,4},{7,5},{8,10},{9,11},{10,... | collective-permute-start | bytes 4616 | tf_op jit(solution)/shard_map/ppermute | solution.py:360
  31.9 2.3 %window_values.3 = (bf16[384,2048]{1,0:T(8,128)(2,1)}, f32[1,384]{1,0:T(1,128)S(1)}) custom-call(bf16[384,256]{1,0:T(8,128)(2,1)S(1)} %copy-done.1, bf16[416,256]{1,0:T(8,128)(2,1)S(1)} %collective-permute-done.v1_ref, bf16[384,256]{1,0:T(8,128)(2,1)S(1)} %collective-permute-done.1.v2_ref, ...), custom_call_target="tpu_custom_call", output_to_operand_aliasing={{0}: (6, {})} | custom-call | flops 1358954496 | bytes 12582912 | tf_op jit(solution)/shard_map/window_values/pallas_call | solution.py:331
  34.2 0.0 collective-permute-done.7
  34.2 0.6 %add_reduce_fusion = f32[384]{0:T(512)} fusion(f32[1,384]{1,0:T(1,128)S(1)} %get-tuple-element.32, f32[1,384]{1,0:T(1,128)S(1)} %collective-permute-done.7), kind=kLoop, calls=%fused_computation.21 | loop fusion | flops 384 | bytes 4608 | tf_op jit(solution)/shard_map/add | solution.py:399
  34.8 0.0 collective-permute-done.8
  34.9 0.6 %reshape_reshape.3 = bf16[1,8,4,2,256]{4,3,2,1,0:T(2,128)(2,1)} reshape(bf16[4,2,8,256]{3,2,1,0:T(8,128)(2,1)S(1)} %pad_maximum_fusion.1) | data formatting | bytes 65536 | tf_op jit(solution)/shard_map/reshape;reshape | solution.py:414
  (25 shorter events, 0.1 us)
Async XLA Ops:
  0.6 13.0 %collective-permute-start.2 = (bf16[384,256]{1,0:T(8,128)(2,1)}, bf16[384,256]{1,0:T(8,128)(2,1)S(1)}, u32[]{:S(2)}, u32[]{:S(2)}) collective-permute-start(bf16[384,256]{1,0:T(8,128)(2,1)} %k_ref.3), channel_id=1, source_target_pairs={{0,8},{4,12},{8,16},{12,20},{16,24},{20,28},{24,0},{28,4},{1,9},{5... | collective-permute-start | bytes 589832 | tf_op jit(solution)/shard_map/ppermute | solution.py:357
  3.7 13.0 %collective-permute-start.3 = (bf16[384,256]{1,0:T(8,128)(2,1)}, bf16[384,256]{1,0:T(8,128)(2,1)S(1)}, u32[]{:S(2)}, u32[]{:S(2)}) collective-permute-start(bf16[384,256]{1,0:T(8,128)(2,1)} %k_ref.3), channel_id=1, source_target_pairs={{0,4},{4,8},{8,12},{12,16},{16,20},{20,24},{24,28},{28,0},{1,5},{5... | collective-permute-start | bytes 589832 | tf_op jit(solution)/shard_map/ppermute | solution.py:357
  5.2 0.9 %copy-start = (bf16[384,256]{1,0:T(8,128)(2,1)S(1)}, bf16[384,256]{1,0:T(8,128)(2,1)}, u32[]{:S(2)}) copy-start(bf16[384,256]{1,0:T(8,128)(2,1)} %v_ref.5) | copy-start | bytes 589828
  6.1 0.9 %copy-start.3 = (bf16[384,256]{1,0:T(8,128)(2,1)S(1)}, bf16[384,256]{1,0:T(8,128)(2,1)}, u32[]{:S(2)}) copy-start(bf16[384,256]{1,0:T(8,128)(2,1)} %k_ref.3) | copy-start | bytes 589828
  7.1 0.7 %copy-start.5 = (s32[1,2,8,4]{2,3,1,0:T(4,128)S(1)}, s32[1,2,8,4]{2,3,1,0:T(4,128)}, u32[]{:S(2)}) copy-start(s32[1,2,8,4]{2,3,1,0:T(4,128)} %param.9) | copy-start | bytes 772
  7.7 0.7 %copy-start.6 = (s32[1,2,8]{2,1,0:T(2,128)S(1)}, s32[1,2,8]{2,1,0:T(2,128)}, u32[]{:S(2)}) copy-start(s32[1,2,8]{2,1,0:T(2,128)} %dest_hbm.1) | copy-start | bytes 196
  8.4 0.7 %copy-start.7 = (s32[1,2,8]{2,1,0:T(2,128)S(1)}, s32[1,2,8]{2,1,0:T(2,128)}, u32[]{:S(2)}) copy-start(s32[1,2,8]{2,1,0:T(2,128)} %live_hbm.1) | copy-start | bytes 196
  9.1 7.6 %copy-start.2 = (bf16[384,2048]{1,0:T(8,128)(2,1)S(1)}, bf16[384,2048]{1,0:T(8,128)(2,1)}, u32[]{:S(2)}) copy-start(bf16[384,2048]{1,0:T(8,128)(2,1)} %q_ref.1) | copy-start | bytes 4718596
  9.1 7.6 %copy-start.4 = (bf16[384,256]{1,0:T(8,128)(2,1)S(1)}, bf16[384,256]{1,0:T(8,128)(2,1)}, u32[]{:S(2)}) copy-start(bf16[384,256]{1,0:T(8,128)(2,1)} %k_ref.3) | copy-start | bytes 589828
  10.5 16.1 %collective-permute-start.1 = (bf16[384,256]{1,0:T(8,128)(2,1)S(1)}, bf16[384,256]{1,0:T(8,128)(2,1)S(1)}, u32[]{:S(2)}, u32[]{:S(2)}) collective-permute-start(bf16[384,256]{1,0:T(8,128)(2,1)S(1)} %get-tuple-element.21), channel_id=1, source_target_pairs={{0,8},{4,12},{8,16},{12,20},{16,24},{20,28},{24,0},{28,4},{1,9},{5... | collective-permute-start | bytes 589832 | tf_op jit(solution)/shard_map/ppermute | solution.py:357
  12.1 12.7 %collective-permute-start = (bf16[416,256]{1,0:T(8,128)(2,1)S(1)}, bf16[416,256]{1,0:T(8,128)(2,1)S(1)}, u32[]{:S(2)}, u32[]{:S(2)}) collective-permute-start(bf16[416,256]{1,0:T(8,128)(2,1)S(1)} %get-tuple-element.20), channel_id=1, source_target_pairs={{0,4},{4,8},{8,12},{12,16},{16,20},{20,24},{24,28},{28,0},{1,5},{5... | collective-permute-start | bytes 638984 | tf_op jit(solution)/shard_map/ppermute | solution.py:357
  13.7 12.9 %copy-start.1 = (bf16[384,256]{1,0:T(8,128)(2,1)S(1)}, bf16[384,256]{1,0:T(8,128)(2,1)}, u32[]{:S(2)}) copy-start(bf16[384,256]{1,0:T(8,128)(2,1)} %v_ref.5) | copy-start | bytes 589828
  23.9 5.2 %collective-permute-start.4 = (f32[1,384]{1,0:T(1,128)S(1)}, f32[1,384]{1,0:T(1,128)S(1)}, u32[]{:S(2)}, u32[]{:S(2)}) collective-permute-start(f32[1,384]{1,0:T(1,128)S(1)} %get-tuple-element.26), channel_id=1, source_target_pairs={{0,28},{4,0},{8,4},{12,8},{16,12},{20,16},{24,20},{28,24},{1,29},{... | collective-permute-start | bytes 4616 | tf_op jit(solution)/shard_map/ppermute | solution.py:357
  24.8 4.3 %collective-permute-start.5 = (f32[40,256]{1,0:T(8,128)S(1)}, f32[40,256]{1,0:T(8,128)S(1)}, u32[]{:S(2)}, u32[]{:S(2)}) collective-permute-start(f32[40,256]{1,0:T(8,128)S(1)} %get-tuple-element.29), channel_id=1, source_target_pairs={{0,24},{4,28},{8,0},{12,4},{16,8},{20,12},{24,16},{28,20},{1,25},{... | collective-permute-start | bytes 122888 | tf_op jit(solution)/shard_map/ppermute | solution.py:357
  29.1 1.2 %collective-permute-start.6 = (f32[1,384]{1,0:T(1,128)S(1)}, f32[1,384]{1,0:T(1,128)S(1)}, u32[]{:S(2)}, u32[]{:S(2)}) collective-permute-start(f32[1,384]{1,0:T(1,128)S(1)} %fusion.1), channel_id=1, source_target_pairs={{0,1},{1,0},{2,3},{3,2},{4,5},{5,4},{6,7},{7,6},{8,9},{9,8},{10,11... | collective-permute-start | bytes 4616 | tf_op jit(solution)/shard_map/ppermute | solution.py:360
  29.2 5.5 %collective-permute-start.8 = (bf16[1,2,2,1,8,256]{5,4,3,2,1,0:T(8,128)(2,1)S(1)}, bf16[1,2,2,1,8,256]{5,4,3,2,1,0:T(8,128)(2,1)S(1)}, u32[]{:S(2)}, u32[]{:S(2)}) collective-permute-start(bf16[1,2,2,1,8,256]{5,4,3,2,1,0:T(8,128)(2,1)S(1)} %broadcast_select_fusion.3), channel_id=1, source_target_pairs={{0,16},{4,20},{8,24},{12,28},{16,0},{20,4},{24,8},{28,12},{1,17},{... | collective-permute-start | bytes 49160 | tf_op jit(solution)/shard_map/ppermute | solution.py:360
  30.3 3.8 %collective-permute-start.7 = (f32[1,384]{1,0:T(1,128)S(1)}, f32[1,384]{1,0:T(1,128)S(1)}, u32[]{:S(2)}, u32[]{:S(2)}) collective-permute-start(f32[1,384]{1,0:T(1,128)S(1)} %add.14.pass_ref), channel_id=1, source_target_pairs={{0,2},{1,3},{2,0},{3,1},{4,6},{5,7},{6,4},{7,5},{8,10},{9,11},{10,... | collective-permute-start | bytes 4616 | tf_op jit(solution)/shard_map/ppermute | solution.py:360

commit v2 on v1

--- a/solution.py
+++ b/solution.py
@@ -93,32 +93,72 @@
 def spans_of(wraps, half):
     if wraps == 0:
         return [(0, 2 * half, 4 * half)]
-    return [(0, half, (3 - wraps) * half), (half, 2 * half, (4 + wraps) * half)]
-
-
-def score_kernel(groups, qpk, half, q_ref, k_ref, k2_ref, k1_ref,
-                 w_ref, inv_ref, own_ref, back1_ref, back2_ref, xkt, bias, s_buf, col):
+    return [(0, half, (4 - wraps) * half if wraps == 1 else 2 * half), (half, 2 * half, (4 + wraps) * half)]
+
+
+def remote_of(wraps, half):
+    return (
+        [(0, 2 * half, 2 * half)],
+        [(0, half, half), (half, 2 * half, 3 * half)],
+        [(half, 2 * half, 4 * half)],
+    )[wraps]
+
+
+def local_kernel(groups, qpk, half, q_ref, k_ref, w_ref, top_ref, sum_ref, xkt, bias, s_buf):
     tok = 2 * half
     steps = qpk // STEP_HEADS
-    edge = tiles(half)
-    late_lo = 3 * half // LANES * LANES
-    late_at = 3 * half - late_lo
+    row = lax.broadcasted_iota(jnp.int32, (tok, tok), 0)
+    column = lax.broadcasted_iota(jnp.int32, (tok, tok), 1)
+    bias[...] = jnp.where(column <= row, 0.0, -jnp.inf)
+    for group in range(groups):
+        xkt[group] = k_ref[:, group * HD : (group + 1) * HD].T
+
+    @pl.loop(0, groups * steps)
+    def _(step):
+        group = step // steps
+
+        def scores(i):
+            at = pl.ds(pl.multiple_of((step * STEP_HEADS + i) * HD, HD), HD)
+            s_buf[i] = jnp.dot(q_ref[:, at], xkt[group], preferred_element_type=jnp.float32)
+
+        def weights(i):
+            head = step * STEP_HEADS + i
+            for r in range(0, tok, CHUNK):
+                rows = slice(r, r + CHUNK)
+                parts = []
+                for at in range(0, tiles(r + CHUNK), LANES):
+                    part = s_buf[i, rows, at : at + LANES]
+                    parts.append(part + bias[rows, at : at + LANES] if at + LANES > r else part)
+                top = wide(jnp.max(functools.reduce(jnp.maximum, parts), axis=1, keepdims=True))
+                parts = [jnp.exp2((part - top) * EXP2_SCALE) for part in parts]
+                top_ref[head, rows] = top
+                sum_ref[head, rows] = wide(
+                    jnp.sum(functools.reduce(jnp.add, parts), axis=1, keepdims=True)
+                )
+                for j, part in enumerate(parts):
+                    w_ref[head, rows, j * LANES : (j + 1) * LANES] = part.astype(jnp.bfloat16)
+
+        scores(0)
+        for i in range(STEP_HEADS):
+            if i + 1 < STEP_HEADS:
+                scores(i + 1)
+            weights(i)
+
+
+def score_kernel(groups, qpk, half, q_ref, k2_ref, k1_ref, wl_ref, top_ref, sum_ref,
+                 w_ref, inv_ref, own_ref, back1_ref, back2_ref, xkt, s_buf, col):
+    tok = 2 * half
+    steps = qpk // STEP_HEADS
     col[...] = jnp.zeros_like(col)
-    row = lax.broadcasted_iota(jnp.int32, (half, edge), 0)
-    column = lax.broadcasted_iota(jnp.int32, (half, edge), 1)
-    masks = ((column >= half) | (column <= row), column <= row, column - late_at <= row)
-    for i, mask in enumerate(masks):
-        bias[i] = jnp.where(mask, 0.0, -jnp.inf)
     cut = jnp.where(lax.broadcasted_iota(jnp.int32, (CHUNK, LANES), 1) < half % LANES, 0.0, -jnp.inf)
     for group in range(groups):
         at = slice(group * HD, (group + 1) * HD)
         xkt[group] = jnp.concatenate(
-            [k_ref[:half, at], k1_ref[:half, at], k2_ref[:half, at],
-             k_ref[half:, at], k2_ref[half:, at], k1_ref[half:, at]], 0
+            [k1_ref[:half, at], k2_ref[:half, at], k2_ref[half:, at], k1_ref[half:, at]], 0
         ).T
 
     def attend(wraps, group, step):
-        spans = spans_of(wraps, half)
+        spans = remote_of(wraps, half)
 
         def scores(i):
             at = pl.ds(pl.multiple_of(((group * steps + step) * STEP_HEADS + i) * HD, HD), HD)
@@ -131,41 +171,50 @@
         def weights(i):
             head = (group * steps + step) * STEP_HEADS + i
             totals = {}
+
+            def add(j, part):
+                part = folded(part)
+                totals[j] = totals[j] + part if j in totals else part
+
+            def merge_local(rows, scale, inverse):
+                inv_ref[head, rows] = inverse
+                live = tiles(rows.stop)
+                for at in range(0, live, LANES):
+                    part = wl_ref[head, rows, at : at + LANES]
+                    if scale is None:
+                        w_ref[head, rows, at : at + LANES] = part
+                        part = part.astype(jnp.float32)
+                    else:
+                        part = part.astype(jnp.float32) * scale
+                        w_ref[head, rows, at : at + LANES] = part.astype(jnp.bfloat16)
+                    add(at // LANES, part * inverse)
+                if live < tok:
+                    w_ref[head, rows, live:tok] = jnp.zeros((CHUNK, tok - live), jnp.bfloat16)
+
+            if wraps == 2:
+                for r in range(0, half, CHUNK):
+                    rows = slice(r, r + CHUNK)
+                    merge_local(rows, None, 1.0 / sum_ref[head, rows])
             for first, last, keys in spans:
                 for r in range(first, last, CHUNK):
                     rows = slice(r, r + CHUNK)
-                    early = r < half
-                    inside = slice(r, r + CHUNK) if early else slice(r - half, r - half + CHUNK)
-                    if early:
-                        valid = (3 - wraps) * half
-                    elif wraps == 0 and inside.stop + 3 * half <= late_lo + LANES:
-                        valid = late_lo + LANES
-                    else:
-                        valid = (4 + wraps) * half
                     parts = []
-                    for at in range(0, valid, LANES):
+                    for at in range(0, keys, LANES):
                         part = s_buf[i, rows, at : at + LANES]
-                        if early and at < edge:
-                            part += bias[1 if wraps == 2 else 0, inside, at : at + LANES]
-                        elif not early and late_lo <= at < late_lo + edge:
-                            part += bias[2, inside, at - late_lo : at - late_lo + LANES]
-                        elif at + LANES > valid:
-                            part += cut
-                        parts.append(part)
-                    peak = wide(jnp.max(functools.reduce(jnp.maximum, parts), axis=1, keepdims=True))
-                    parts = [jnp.exp2((part - peak) * EXP2_SCALE) for part in parts]
-                    inverse = 1.0 / wide(
-                        jnp.sum(functools.reduce(jnp.add, parts), axis=1, keepdims=True)
-                    )
-                    inv_ref[head, rows] = inverse
+                        parts.append(part + cut if at + LANES > keys else part)
+                    top = wide(jnp.max(functools.reduce(jnp.maximum, parts), axis=1, keepdims=True))
+                    top_l = top_ref[head, rows]
+                    top = jnp.maximum(top, top_l)
+                    scale = jnp.exp2((top_l - top) * EXP2_SCALE)
+                    parts = [jnp.exp2((part - top) * EXP2_SCALE) for part in parts]
+                    total = wide(jnp.sum(functools.reduce(jnp.add, parts), axis=1, keepdims=True))
+                    inverse = 1.0 / (sum_ref[head, rows] * scale + total)
                     for j, part in enumerate(parts):
-                        w_ref[head, rows, j * LANES : (j + 1) * LANES] = part.astype(jnp.bfloat16)
-                        part = folded(part * inverse)
-                        totals[j] = totals[j] + part if j in totals else part
-                    if len(parts) * LANES < tiles(keys):
-                        w_ref[head, rows, len(parts) * LANES : tiles(keys)] = jnp.zeros(
-                            (CHUNK, tiles(keys) - len(parts) * LANES), jnp.bfloat16
+                        w_ref[head, rows, tok + j * LANES : tok + (j + 1) * LANES] = part.astype(
+                            jnp.bfloat16
                         )
+                        add(tok // LANES + j, part * inverse)
+                    merge_local(rows, scale, inverse)
             for j, block in totals.items():
                 col[:, j * LANES : (j + 1) * LANES] += block
 
@@ -181,12 +230,10 @@
             pl.loop(0, steps)(functools.partial(attend, wraps, group))
 
     total = jnp.sum(col[...], axis=0, keepdims=True) * (1.0 / QH)
-    own_ref[:, :half] = total[:, :half]
-    own_ref[:, half:] = total[:, 3 * half : 4 * half]
-    back1_ref[:, :half] = total[:, half : 2 * half]
-    back1_ref[:, half:] = total[:, 5 * half :]
-    back2_ref[:, :half] = total[:, 2 * half : 3 * half]
-    back2_ref[:, half:] = total[:, 4 * half : 5 * half]
+    own_ref[...] = total[:, :tok]
+    back1_ref[:, :half] = total[:, tok : tok + half]
+    back1_ref[:, half:] = total[:, tok + 3 * half :]
+    back2_ref[...] = total[:, tok + half : tok + 3 * half]
 
 
 def value_kernel(group, qpk, half, v_ref, v1_ref, v2_ref, w_ref, inv_ref, pass_ref, *refs):
@@ -196,8 +243,7 @@
     again_ref[...] = pass_ref[...]
     at = slice(group * HD, (group + 1) * HD)
     xv[...] = jnp.concatenate(
-        [v_ref[:half, at], v1_ref[:half, at], v2_ref[:half, at],
-         v_ref[half:, at], v2_ref[half:, at], v1_ref[half:tok, at]], 0
+        [v_ref[:, at], v1_ref[:half, at], v2_ref[:half, at], v2_ref[half:, at], v1_ref[half:tok, at]], 0
     )
 
     def sent(step):
@@ -260,33 +306,53 @@
     )(keys, values, *kept)
 
 
-def window_scores(queries, keys, k2, k1):
+def local_scores(queries, keys):
+    tok, width = queries.shape
+    groups = keys.shape[1] // HD
+    heads = width // HD
+    spread = jax.ShapeDtypeStruct((heads, tok, LANES), jnp.float32)
+    return pl.pallas_call(
+        functools.partial(local_kernel, groups, heads // groups, tok // 2),
+        out_shape=(jax.ShapeDtypeStruct((heads, tok, tok), jnp.bfloat16), spread, spread),
+        in_specs=[VMEM] * 2,
+        out_specs=(VMEM,) * 3,
+        scratch_shapes=[
+            pltpu.VMEM((groups, HD, tok), jnp.bfloat16),
+            pltpu.VMEM((tok, tok), jnp.float32),
+            pltpu.VMEM((STEP_HEADS, tok, tok), jnp.float32),
+        ],
+        compiler_params=pltpu.CompilerParams(vmem_limit_bytes=12 * MIB),
+        cost_estimate=cost(3, heads, tok // 2),
+        name="local_scores",
+    )(queries, keys)
+
+
+def remote_scores(queries, k2, k1, *local):
     tok, width = queries.shape
     half = tok // 2
-    groups = keys.shape[1] // HD
+    groups = k1.shape[1] // HD
     heads = width // HD
-    most = 6 * half
+    line = jax.ShapeDtypeStruct((1, tok), jnp.float32)
     return pl.pallas_call(
         functools.partial(score_kernel, groups, heads // groups, half),
         out_shape=(
-            jax.ShapeDtypeStruct((heads, tok, most), jnp.bfloat16),
+            jax.ShapeDtypeStruct((heads, tok, 6 * half), jnp.bfloat16),
             jax.ShapeDtypeStruct((heads, tok, LANES), jnp.float32),
-            jax.ShapeDtypeStruct((1, tok), jnp.float32),
-            jax.ShapeDtypeStruct((1, tok), jnp.float32),
-            jax.ShapeDtypeStruct((1, tok), jnp.float32),
+            line,
+            line,
+            line,
         ),
-        in_specs=[VMEM] * 4,
+        in_specs=[VMEM] * 6,
         out_specs=(VMEM,) * 5,
         scratch_shapes=[
-            pltpu.VMEM((groups, HD, most), jnp.bfloat16),
-            pltpu.VMEM((3, half, tiles(half)), jnp.float32),
-            pltpu.VMEM((STEP_HEADS, tok, most), jnp.float32),
-            pltpu.VMEM((8, most), jnp.float32),
+            pltpu.VMEM((groups, HD, 4 * half), jnp.bfloat16),
+            pltpu.VMEM((STEP_HEADS, tok, 4 * half), jnp.float32),
+            pltpu.VMEM((8, 6 * half), jnp.float32),
         ],
-        compiler_params=pltpu.CompilerParams(vmem_limit_bytes=20 * MIB),
-        cost_estimate=cost(7, heads, half),
-        name="window_scores",
-    )(queries, keys, k2, k1)
+        compiler_params=pltpu.CompilerParams(vmem_limit_bytes=16 * MIB),
+        cost_estimate=cost(4, heads, half),
+        name="remote_scores",
+    )(queries, k2, k1, *local)
 
 
 def ride(back, kept, v1):
@@ -366,7 +432,9 @@
     )
     v1 = along(again1, 1)
     v2 = along(again2, 2)
-    weights, inverse, own, back1, back2 = window_scores(queries, keys, k2, k1)
+    weights, inverse, own, back1, back2 = remote_scores(
+        queries, k2, k1, *local_scores(queries, keys)
+    )
     tok = keys.shape[0]
     riding, stay = ride(back2, kept, v1)
     back1, riding = along(back1, -1), along(riding, -2)

time: 35.7 us -> 36.5 us (1.022)
  waiting for transfers between devices: 4.51 us -> 1.6 us
  Pallas kernels: 13.3 us -> 15.2 us
  starting transfers between devices: 11.7 us -> 13.4 us
    ppermute x6, waiting for transfers between devices: 3.93 us -> 1.04 us  [along(): lax.ppermute(block, 'ctx', [(i, (i + distance) % count) for i in range(co...]
    ppermute x6, starting transfers between devices: 9.56 us -> 11.3 us  [along(): lax.ppermute(block, 'ctx', [(i, (i + distance) % count) for i in range(co...]
    pallas_call x1 -> x2, Pallas kernels: 7.15 us -> 8.81 us  [the longest x1 5.77 us: remote_scores(): pl.pallas_call(functools.partial(score_kernel, groups, heads // groups, h...]
  transfers between devices with their start and end apart: 9 -> 9, of which waited for: 3 -> 3; matrix products, arithmetic and copies ran while one was open for 2% -> 2% of each run, Pallas kernels for 37% -> 42%
where the time goes in v2:
time: 36.5 us; the launch traced here: 36.3 us
  Pallas kernels  15.2 us (42%)
  starting transfers between devices  13.4 us (37%)
  local copies, waits for them, and re-layouts  4.56 us (12%)
  waiting for transfers between devices  1.6 us (4%)
  between operations  0.8 us (2%)
  other arithmetic  0.67 us (2%)
    ppermute x6, starting transfers between devices, along(): lax.ppermute(block, 'ctx', [(i, (i + distance) % count) for i in range(co...  11.3 us
    pallas_call x1, Pallas kernels, remote_scores(): pl.pallas_call(functools.partial(score_kernel, groups, heads // groups, h...  5.77 us
    pallas_call x2, Pallas kernels, window_values(): pl.pallas_call(functools.partial(value_kernel, group, heads // groups, to...  5.07 us
    unnamed x16, local copies, waits for them, and re-layouts  3.91 us
    pallas_call x1, Pallas kernels, local_scores(): pl.pallas_call(functools.partial(local_kernel, groups, heads // groups, t...  3.03 us
    ppermute x3, starting transfers between devices, swap(): lax.ppermute(block, axis, [(i, i ^ bit) for i in range(lax.axis_size(axis...  2.14 us
    pallas_call x1, Pallas kernels, keep(): pl.pallas_call(functools.partial(keep_kernel, groups), out_shape=shapes,...  1.35 us
    ppermute x6, waiting for transfers between devices, along(): lax.ppermute(block, 'ctx', [(i, (i + distance) % count) for i in range(co...  1.04 us
  transfers between devices with their start and end apart: 9, of which 3 were waited for; matrix products, arithmetic and copies ran while one was open for 2% of the time, Pallas kernels for 42%

profile of v2, /device:TPU:0, one launch (start us, length us, event | category | flops | bytes accessed | tf_op | source)
XLA Modules:
  0.0 36.3 jit_solution(16867239038072494149)
XLA Ops:
  0.6 3.1 %collective-permute-start.2 = (bf16[384,256]{1,0:T(8,128)(2,1)}, bf16[384,256]{1,0:T(8,128)(2,1)S(1)}, u32[]{:S(2)}, u32[]{:S(2)}) collective-permute-start(bf16[384,256]{1,0:T(8,128)(2,1)} %k_ref.3), channel_id=1, source_target_pairs={{0,8},{4,12},{8,16},{12,20},{16,24},{20,28},{24,0},{28,4},{1,9},{5... | collective-permute-start | bytes 589832 | tf_op jit(solution)/shard_map/ppermute | solution.py:423
  3.7 1.5 %collective-permute-start.3 = (bf16[384,256]{1,0:T(8,128)(2,1)}, bf16[384,256]{1,0:T(8,128)(2,1)S(1)}, u32[]{:S(2)}, u32[]{:S(2)}) collective-permute-start(bf16[384,256]{1,0:T(8,128)(2,1)} %k_ref.3), channel_id=1, source_target_pairs={{0,4},{4,8},{8,12},{12,16},{16,20},{20,24},{24,28},{28,0},{1,5},{5... | collective-permute-start | bytes 589832 | tf_op jit(solution)/shard_map/ppermute | solution.py:423
  5.2 0.9 %copy-done = bf16[384,256]{1,0:T(8,128)(2,1)S(1)} copy-done((bf16[384,256]{1,0:T(8,128)(2,1)S(1)}, bf16[384,256]{1,0:T(8,128)(2,1)}, u32[]{:S(2)}) %copy-start) | copy-done | bytes 196632
  6.1 0.9 %copy-done.3 = bf16[384,256]{1,0:T(8,128)(2,1)S(1)} copy-done((bf16[384,256]{1,0:T(8,128)(2,1)S(1)}, bf16[384,256]{1,0:T(8,128)(2,1)}, u32[]{:S(2)}) %copy-start.3) | copy-done | bytes 196632
  7.1 0.7 %copy-done.5 = s32[1,2,8,4]{2,3,1,0:T(4,128)S(1)} copy-done((s32[1,2,8,4]{2,3,1,0:T(4,128)S(1)}, s32[1,2,8,4]{2,3,1,0:T(4,128)}, u32[]{:S(2)}) %copy-start.5) | copy-done | bytes 280
  7.7 0.7 %copy-done.6 = s32[1,2,8]{2,1,0:T(2,128)S(1)} copy-done((s32[1,2,8]{2,1,0:T(2,128)S(1)}, s32[1,2,8]{2,1,0:T(2,128)}, u32[]{:S(2)}) %copy-start.6) | copy-done | bytes 88
  8.4 0.7 %copy-done.7 = s32[1,2,8]{2,1,0:T(2,128)S(1)} copy-done((s32[1,2,8]{2,1,0:T(2,128)S(1)}, s32[1,2,8]{2,1,0:T(2,128)}, u32[]{:S(2)}) %copy-start.7) | copy-done | bytes 88
  9.1 1.3 %keep_rows.1 = (bf16[32,256]{1,0:T(8,128)(2,1)S(1)}, bf16[416,256]{1,0:T(8,128)(2,1)S(1)}, bf16[384,256]{1,0:T(8,128)(2,1)S(1)}, s32[8,256]{1,0:T(8,128)S(1)}, s...) custom-call(bf16[384,256]{1,0:T(8,128)(2,1)S(1)} %copy-done.3, bf16[384,256]{1,0:T(8,128)(2,1)S(1)} %copy-done, ...), custom_call_target="tpu_custom_call" | custom-call | flops 1811939328 | bytes 25165824 | tf_op jit(solution)/shard_map/keep_rows/pallas_call | solution.py:296
  10.5 1.6 %collective-permute-start = (bf16[416,256]{1,0:T(8,128)(2,1)S(1)}, bf16[416,256]{1,0:T(8,128)(2,1)S(1)}, u32[]{:S(2)}, u32[]{:S(2)}) collective-permute-start(bf16[416,256]{1,0:T(8,128)(2,1)S(1)} %get-tuple-element.23), channel_id=1, source_target_pairs={{0,4},{4,8},{8,12},{12,16},{16,20},{20,24},{24,28},{28,0},{1,5},{5... | collective-permute-start | bytes 638984 | tf_op jit(solution)/shard_map/ppermute | solution.py:423
  12.1 1.6 %collective-permute-start.1 = (bf16[384,256]{1,0:T(8,128)(2,1)S(1)}, bf16[384,256]{1,0:T(8,128)(2,1)S(1)}, u32[]{:S(2)}, u32[]{:S(2)}) collective-permute-start(bf16[384,256]{1,0:T(8,128)(2,1)S(1)} %get-tuple-element.24), channel_id=1, source_target_pairs={{0,8},{4,12},{8,16},{12,20},{16,24},{20,28},{24,0},{28,4},{1,9},{5... | collective-permute-start | bytes 589832 | tf_op jit(solution)/shard_map/ppermute | solution.py:423
  13.6 0.0 copy-done.2
  13.6 3.0 %local_scores.1 = (bf16[16,384,384]{2,1,0:T(8,128)(2,1)S(1)}, f32[16,384,128]{2,1,0:T(8,128)S(1)}, f32[16,384,128]{2,1,0:T(8,128)S(1)}) custom-call(bf16[384,2048]{1,0:T(8,128)(2,1)S(1)} %copy-done.2, bf16[384,256]{1,0:T(8,128)(2,1)S(1)} %copy-done.4), custom_call_target="tpu_custom_call" | custom-call | flops 2717908992 | bytes 25165824 | tf_op jit(solution)/shard_map/local_scores/pallas_call | solution.py:314
  16.7 0.0 collective-permute-done.2.k2_ref
  16.7 0.1 collective-permute-done.3.k1_ref
  16.8 5.8 %remote_scores.1 = (bf16[16,384,1152]{2,1,0:T(8,128)(2,1)S(1)}, f32[16,384,128]{2,1,0:T(8,128)S(1)}, f32[1,384]{1,0:T(1,128)S(1)}, f32[1,384]{1,0:T(1,128)S(1)}, f32[1,384]{1,0:T(1,128)S(1)}) custom-call(bf16[384,2048]{1,0:T(8,128)(2,1)S(1)} %copy-done.2, bf16[384,256]{1,0:T(8,128)(2,1)S(1)} %collective-permute-done.2.k2_ref, ...), custom_call_target="tpu_custom_call" | custom-call | flops 3623878656 | bytes 25165824 | tf_op jit(solution)/shard_map/remote_scores/pallas_call | solution.py:336
  22.6 3.0 %collective-permute-start.4 = (f32[1,384]{1,0:T(1,128)S(1)}, f32[1,384]{1,0:T(1,128)S(1)}, u32[]{:S(2)}, u32[]{:S(2)}) collective-permute-start(f32[1,384]{1,0:T(1,128)S(1)} %get-tuple-element.32), channel_id=1, source_target_pairs={{0,28},{4,0},{8,4},{12,8},{16,12},{20,16},{24,20},{28,24},{1,29},{... | collective-permute-start | bytes 4616 | tf_op jit(solution)/shard_map/ppermute | solution.py:423
  25.6 0.0 collective-permute-done.v1_ref
  25.6 0.5 %collective-permute-start.5 = (f32[40,256]{1,0:T(8,128)S(1)}, f32[40,256]{1,0:T(8,128)S(1)}, u32[]{:S(2)}, u32[]{:S(2)}) collective-permute-start(f32[40,256]{1,0:T(8,128)S(1)} %get-tuple-element.35), channel_id=1, source_target_pairs={{0,24},{4,28},{8,0},{12,4},{16,8},{20,12},{24,16},{28,20},{1,25},{... | collective-permute-start | bytes 122888 | tf_op jit(solution)/shard_map/ppermute | solution.py:423
  26.1 0.0 collective-permute-done.1.v2_ref
  26.1 0.0 copy-done.1
  26.2 2.6 %window_values.2 = (bf16[384,2048]{1,0:T(8,128)(2,1)}, f32[1,384]{1,0:T(1,128)S(1)}) custom-call(bf16[384,256]{1,0:T(8,128)(2,1)S(1)} %copy-done.1, bf16[416,256]{1,0:T(8,128)(2,1)S(1)} %collective-permute-done.v1_ref, bf16[384,256]{1,0:T(8,128)(2,1)S(1)} %collective-permute-done.1.v2_ref, bf16[16,384,1152]{2,1,0:T(8,128)(2,1)S(1)} %get-tuple-element.28.w_ref, ...), custom_call_target="tpu_custom_call" | custom-call | flops 1358954496 | bytes 12582912 | tf_op jit(solution)/shard_map/window_values/pallas_call | solution.py:397
  28.8 0.9 %collective-permute-done.5 = f32[40,256]{1,0:T(8,128)S(1)} collective-permute-done((f32[40,256]{1,0:T(8,128)S(1)}, f32[40,256]{1,0:T(8,128)S(1)}, u32[]{:S(2)}, u32[]{:S(2)}) %collective-permute-start.5) | collective-permute-done | bytes 40992 | tf_op jit(solution)/shard_map/ppermute | solution.py:423
  29.7 0.0 collective-permute-done.4
  29.7 0.1 collective-permute-start.6
  29.8 0.5 %collective-permute-start.8 = (bf16[1,2,2,1,8,256]{5,4,3,2,1,0:T(8,128)(2,1)S(1)}, bf16[1,2,2,1,8,256]{5,4,3,2,1,0:T(8,128)(2,1)S(1)}, u32[]{:S(2)}, u32[]{:S(2)}) collective-permute-start(bf16[1,2,2,1,8,256]{5,4,3,2,1,0:T(8,128)(2,1)S(1)} %broadcast_select_fusion.3), channel_id=1, source_target_pairs={{0,16},{4,20},{8,24},{12,28},{16,0},{20,4},{24,8},{28,12},{1,17},{... | collective-permute-start | bytes 49160 | tf_op jit(solution)/shard_map/ppermute | solution.py:426
  30.4 0.6 %collective-permute-done.6 = f32[1,384]{1,0:T(1,128)S(1)} collective-permute-done((f32[1,384]{1,0:T(1,128)S(1)}, f32[1,384]{1,0:T(1,128)S(1)}, u32[]{:S(2)}, u32[]{:S(2)}) %collective-permute-start.6) | collective-permute-done | bytes 1568 | tf_op jit(solution)/shard_map/ppermute | solution.py:426
  30.9 1.5 %collective-permute-start.7 = (f32[1,384]{1,0:T(1,128)S(1)}, f32[1,384]{1,0:T(1,128)S(1)}, u32[]{:S(2)}, u32[]{:S(2)}) collective-permute-start(f32[1,384]{1,0:T(1,128)S(1)} %add.14.pass_ref), channel_id=1, source_target_pairs={{0,2},{1,3},{2,0},{3,1},{4,6},{5,7},{6,4},{7,5},{8,10},{9,11},{10,... | collective-permute-start | bytes 4616 | tf_op jit(solution)/shard_map/ppermute | solution.py:426
  32.5 2.4 %window_values.3 = (bf16[384,2048]{1,0:T(8,128)(2,1)}, f32[1,384]{1,0:T(1,128)S(1)}) custom-call(bf16[384,256]{1,0:T(8,128)(2,1)S(1)} %copy-done.1, bf16[416,256]{1,0:T(8,128)(2,1)S(1)} %collective-permute-done.v1_ref, bf16[384,256]{1,0:T(8,128)(2,1)S(1)} %collective-permute-done.1.v2_ref, ...), custom_call_target="tpu_custom_call", output_to_operand_aliasing={{0}: (6, {})} | custom-call | flops 1358954496 | bytes 12582912 | tf_op jit(solution)/shard_map/window_values/pallas_call | solution.py:397
  34.9 0.0 collective-permute-done.7
  34.9 0.6 %add_reduce_fusion = f32[384]{0:T(512)} fusion(f32[1,384]{1,0:T(1,128)S(1)} %get-tuple-element.38, f32[1,384]{1,0:T(1,128)S(1)} %collective-permute-done.7), kind=kLoop, calls=%fused_computation.21 | loop fusion | flops 384 | bytes 4608 | tf_op jit(solution)/shard_map/add | solution.py:467
  35.5 0.0 collective-permute-done.8
  35.6 0.6 %reshape_reshape.3 = bf16[1,8,4,2,256]{4,3,2,1,0:T(2,128)(2,1)} reshape(bf16[4,2,8,256]{3,2,1,0:T(8,128)(2,1)S(1)} %pad_maximum_fusion.1) | data formatting | bytes 65536 | tf_op jit(solution)/shard_map/reshape;reshape | solution.py:482
  (26 shorter events, 0.1 us)
Async XLA Ops:
  0.6 16.1 %collective-permute-start.2 = (bf16[384,256]{1,0:T(8,128)(2,1)}, bf16[384,256]{1,0:T(8,128)(2,1)S(1)}, u32[]{:S(2)}, u32[]{:S(2)}) collective-permute-start(bf16[384,256]{1,0:T(8,128)(2,1)} %k_ref.3), channel_id=1, source_target_pairs={{0,8},{4,12},{8,16},{12,20},{16,24},{20,28},{24,0},{28,4},{1,9},{5... | collective-permute-start | bytes 589832 | tf_op jit(solution)/shard_map/ppermute | solution.py:423
  3.7 13.1 %collective-permute-start.3 = (bf16[384,256]{1,0:T(8,128)(2,1)}, bf16[384,256]{1,0:T(8,128)(2,1)S(1)}, u32[]{:S(2)}, u32[]{:S(2)}) collective-permute-start(bf16[384,256]{1,0:T(8,128)(2,1)} %k_ref.3), channel_id=1, source_target_pairs={{0,4},{4,8},{8,12},{12,16},{16,20},{20,24},{24,28},{28,0},{1,5},{5... | collective-permute-start | bytes 589832 | tf_op jit(solution)/shard_map/ppermute | solution.py:423
  5.2 0.9 %copy-start = (bf16[384,256]{1,0:T(8,128)(2,1)S(1)}, bf16[384,256]{1,0:T(8,128)(2,1)}, u32[]{:S(2)}) copy-start(bf16[384,256]{1,0:T(8,128)(2,1)} %v_ref.5) | copy-start | bytes 589828
  6.1 0.9 %copy-start.3 = (bf16[384,256]{1,0:T(8,128)(2,1)S(1)}, bf16[384,256]{1,0:T(8,128)(2,1)}, u32[]{:S(2)}) copy-start(bf16[384,256]{1,0:T(8,128)(2,1)} %k_ref.3) | copy-start | bytes 589828
  7.1 0.7 %copy-start.5 = (s32[1,2,8,4]{2,3,1,0:T(4,128)S(1)}, s32[1,2,8,4]{2,3,1,0:T(4,128)}, u32[]{:S(2)}) copy-start(s32[1,2,8,4]{2,3,1,0:T(4,128)} %param.9) | copy-start | bytes 772
  7.7 0.7 %copy-start.6 = (s32[1,2,8]{2,1,0:T(2,128)S(1)}, s32[1,2,8]{2,1,0:T(2,128)}, u32[]{:S(2)}) copy-start(s32[1,2,8]{2,1,0:T(2,128)} %dest_hbm.1) | copy-start | bytes 196
  8.4 0.7 %copy-start.7 = (s32[1,2,8]{2,1,0:T(2,128)S(1)}, s32[1,2,8]{2,1,0:T(2,128)}, u32[]{:S(2)}) copy-start(s32[1,2,8]{2,1,0:T(2,128)} %live_hbm.1) | copy-start | bytes 196
  9.1 4.5 %copy-start.2 = (bf16[384,2048]{1,0:T(8,128)(2,1)S(1)}, bf16[384,2048]{1,0:T(8,128)(2,1)}, u32[]{:S(2)}) copy-start(bf16[384,2048]{1,0:T(8,128)(2,1)} %q_ref.3) | copy-start | bytes 4718596
  9.1 4.5 %copy-start.4 = (bf16[384,256]{1,0:T(8,128)(2,1)S(1)}, bf16[384,256]{1,0:T(8,128)(2,1)}, u32[]{:S(2)}) copy-start(bf16[384,256]{1,0:T(8,128)(2,1)} %k_ref.3) | copy-start | bytes 589828
  10.5 15.2 %collective-permute-start = (bf16[416,256]{1,0:T(8,128)(2,1)S(1)}, bf16[416,256]{1,0:T(8,128)(2,1)S(1)}, u32[]{:S(2)}, u32[]{:S(2)}) collective-permute-start(bf16[416,256]{1,0:T(8,128)(2,1)S(1)} %get-tuple-element.23), channel_id=1, source_target_pairs={{0,4},{4,8},{8,12},{12,16},{16,20},{20,24},{24,28},{28,0},{1,5},{5... | collective-permute-start | bytes 638984 | tf_op jit(solution)/shard_map/ppermute | solution.py:423
  12.1 14.1 %collective-permute-start.1 = (bf16[384,256]{1,0:T(8,128)(2,1)S(1)}, bf16[384,256]{1,0:T(8,128)(2,1)S(1)}, u32[]{:S(2)}, u32[]{:S(2)}) collective-permute-start(bf16[384,256]{1,0:T(8,128)(2,1)S(1)} %get-tuple-element.24), channel_id=1, source_target_pairs={{0,8},{4,12},{8,16},{12,20},{16,24},{20,28},{24,0},{28,4},{1,9},{5... | collective-permute-start | bytes 589832 | tf_op jit(solution)/shard_map/ppermute | solution.py:423
  16.8 9.3 %copy-start.1 = (bf16[384,256]{1,0:T(8,128)(2,1)S(1)}, bf16[384,256]{1,0:T(8,128)(2,1)}, u32[]{:S(2)}) copy-start(bf16[384,256]{1,0:T(8,128)(2,1)} %v_ref.5) | copy-start | bytes 589828
  22.6 7.1 %collective-permute-start.4 = (f32[1,384]{1,0:T(1,128)S(1)}, f32[1,384]{1,0:T(1,128)S(1)}, u32[]{:S(2)}, u32[]{:S(2)}) collective-permute-start(f32[1,384]{1,0:T(1,128)S(1)} %get-tuple-element.32), channel_id=1, source_target_pairs={{0,28},{4,0},{8,4},{12,8},{16,12},{20,16},{24,20},{28,24},{1,29},{... | collective-permute-start | bytes 4616 | tf_op jit(solution)/shard_map/ppermute | solution.py:423
  25.6 4.1 %collective-permute-start.5 = (f32[40,256]{1,0:T(8,128)S(1)}, f32[40,256]{1,0:T(8,128)S(1)}, u32[]{:S(2)}, u32[]{:S(2)}) collective-permute-start(f32[40,256]{1,0:T(8,128)S(1)} %get-tuple-element.35), channel_id=1, source_target_pairs={{0,24},{4,28},{8,0},{12,4},{16,8},{20,12},{24,16},{28,20},{1,25},{... | collective-permute-start | bytes 122888 | tf_op jit(solution)/shard_map/ppermute | solution.py:423
  29.7 1.2 %collective-permute-start.6 = (f32[1,384]{1,0:T(1,128)S(1)}, f32[1,384]{1,0:T(1,128)S(1)}, u32[]{:S(2)}, u32[]{:S(2)}) collective-permute-start(f32[1,384]{1,0:T(1,128)S(1)} %fusion.1), channel_id=1, source_target_pairs={{0,1},{1,0},{2,3},{3,2},{4,5},{5,4},{6,7},{7,6},{8,9},{9,8},{10,11... | collective-permute-start | bytes 4616 | tf_op jit(solution)/shard_map/ppermute | solution.py:426
  29.8 5.7 %collective-permute-start.8 = (bf16[1,2,2,1,8,256]{5,4,3,2,1,0:T(8,128)(2,1)S(1)}, bf16[1,2,2,1,8,256]{5,4,3,2,1,0:T(8,128)(2,1)S(1)}, u32[]{:S(2)}, u32[]{:S(2)}) collective-permute-start(bf16[1,2,2,1,8,256]{5,4,3,2,1,0:T(8,128)(2,1)S(1)} %broadcast_select_fusion.3), channel_id=1, source_target_pairs={{0,16},{4,20},{8,24},{12,28},{16,0},{20,4},{24,8},{28,12},{1,17},{... | collective-permute-start | bytes 49160 | tf_op jit(solution)/shard_map/ppermute | solution.py:426
  30.9 4.0 %collective-permute-start.7 = (f32[1,384]{1,0:T(1,128)S(1)}, f32[1,384]{1,0:T(1,128)S(1)}, u32[]{:S(2)}, u32[]{:S(2)}) collective-permute-start(f32[1,384]{1,0:T(1,128)S(1)} %add.14.pass_ref), channel_id=1, source_target_pairs={{0,2},{1,3},{2,0},{3,1},{4,6},{5,7},{6,4},{7,5},{8,10},{9,11},{10,... | collective-permute-start | bytes 4616 | tf_op jit(solution)/shard_map/ppermute | solution.py:426

commit v3 on v2

--- a/solution.py
+++ b/solution.py
@@ -13,7 +13,9 @@
 QH = 64
 LANES = 128
 CHUNK = 32
-STEP_HEADS = 4
+STEP_HEADS = 8
+SLOTS = 4
+OUT_HEADS = 2
 EXP2_SCALE = HD ** (-0.5) * math.log2(math.e)
 VMEM = pl.BlockSpec(memory_space=pltpu.VMEM)
 HBM = pl.BlockSpec(memory_space=pltpu.HBM)
@@ -96,75 +98,76 @@
     return [(0, half, (4 - wraps) * half if wraps == 1 else 2 * half), (half, 2 * half, (4 + wraps) * half)]
 
 
-def remote_of(wraps, half):
-    return (
-        [(0, 2 * half, 2 * half)],
-        [(0, half, half), (half, 2 * half, 3 * half)],
-        [(half, 2 * half, 4 * half)],
-    )[wraps]
-
-
 def local_kernel(groups, qpk, half, q_ref, k_ref, w_ref, top_ref, sum_ref, xkt, bias, s_buf):
     tok = 2 * half
     steps = qpk // STEP_HEADS
+    @pl.when(lax.axis_index("ctx") == 0)
+    def _():
+        row = lax.broadcasted_iota(jnp.int32, (tok, tok), 0)
+        column = lax.broadcasted_iota(jnp.int32, (tok, tok), 1)
+        bias[...] = jnp.where(column <= row, 0.0, -jnp.inf)
+        for group in range(groups):
+            xkt[group] = k_ref[:, group * HD : (group + 1) * HD].T
+
+        @pl.loop(0, groups * steps)
+        def _(step):
+            group = step // steps
+
+            def scores(i):
+                at = pl.ds(pl.multiple_of((step * STEP_HEADS + i) * HD, HD), HD)
+                s_buf[i % SLOTS] = jnp.dot(q_ref[:, at], xkt[group], preferred_element_type=jnp.float32)
+
+            def weights(i):
+                head = step * STEP_HEADS + i
+                for r in range(0, tok, CHUNK):
+                    rows = slice(r, r + CHUNK)
+                    parts = []
+                    for at in range(0, tiles(r + CHUNK), LANES):
+                        part = s_buf[i % SLOTS, rows, at : at + LANES]
+                        parts.append(part + bias[rows, at : at + LANES] if at + LANES > r else part)
+                    top = wide(jnp.max(functools.reduce(jnp.maximum, parts), axis=1, keepdims=True))
+                    parts = [jnp.exp2((part - top) * EXP2_SCALE) for part in parts]
+                    top_ref[head, rows] = top
+                    sum_ref[head, rows] = wide(
+                        jnp.sum(functools.reduce(jnp.add, parts), axis=1, keepdims=True)
+                    )
+                    for j, part in enumerate(parts):
+                        w_ref[head, rows, j * LANES : (j + 1) * LANES] = part.astype(jnp.bfloat16)
+
+            scores(0)
+            for i in range(STEP_HEADS):
+                if i + 1 < STEP_HEADS:
+                    scores(i + 1)
+                weights(i)
+
+
+def score_kernel(groups, qpk, half, q_ref, k_ref, k2_ref, k1_ref, wl_ref, top_ref, sum_ref,
+                 w_ref, inv_ref, own_ref, back1_ref, back2_ref, xkt, bias, s_buf, col):
+    tok = 2 * half
+    steps = qpk // STEP_HEADS
+    col[...] = jnp.zeros_like(col)
     row = lax.broadcasted_iota(jnp.int32, (tok, tok), 0)
     column = lax.broadcasted_iota(jnp.int32, (tok, tok), 1)
     bias[...] = jnp.where(column <= row, 0.0, -jnp.inf)
-    for group in range(groups):
-        xkt[group] = k_ref[:, group * HD : (group + 1) * HD].T
-
-    @pl.loop(0, groups * steps)
-    def _(step):
-        group = step // steps
-
-        def scores(i):
-            at = pl.ds(pl.multiple_of((step * STEP_HEADS + i) * HD, HD), HD)
-            s_buf[i] = jnp.dot(q_ref[:, at], xkt[group], preferred_element_type=jnp.float32)
-
-        def weights(i):
-            head = step * STEP_HEADS + i
-            for r in range(0, tok, CHUNK):
-                rows = slice(r, r + CHUNK)
-                parts = []
-                for at in range(0, tiles(r + CHUNK), LANES):
-                    part = s_buf[i, rows, at : at + LANES]
-                    parts.append(part + bias[rows, at : at + LANES] if at + LANES > r else part)
-                top = wide(jnp.max(functools.reduce(jnp.maximum, parts), axis=1, keepdims=True))
-                parts = [jnp.exp2((part - top) * EXP2_SCALE) for part in parts]
-                top_ref[head, rows] = top
-                sum_ref[head, rows] = wide(
-                    jnp.sum(functools.reduce(jnp.add, parts), axis=1, keepdims=True)
-                )
-                for j, part in enumerate(parts):
-                    w_ref[head, rows, j * LANES : (j + 1) * LANES] = part.astype(jnp.bfloat16)
-
-        scores(0)
-        for i in range(STEP_HEADS):
-            if i + 1 < STEP_HEADS:
-                scores(i + 1)
-            weights(i)
-
-
-def score_kernel(groups, qpk, half, q_ref, k2_ref, k1_ref, wl_ref, top_ref, sum_ref,
-                 w_ref, inv_ref, own_ref, back1_ref, back2_ref, xkt, s_buf, col):
-    tok = 2 * half
-    steps = qpk // STEP_HEADS
-    col[...] = jnp.zeros_like(col)
     cut = jnp.where(lax.broadcasted_iota(jnp.int32, (CHUNK, LANES), 1) < half % LANES, 0.0, -jnp.inf)
     for group in range(groups):
         at = slice(group * HD, (group + 1) * HD)
         xkt[group] = jnp.concatenate(
-            [k1_ref[:half, at], k2_ref[:half, at], k2_ref[half:, at], k1_ref[half:, at]], 0
+            [k_ref[:, at], k1_ref[:half, at], k2_ref[:half, at], k2_ref[half:, at], k1_ref[half:, at]], 0
         ).T
 
     def attend(wraps, group, step):
-        spans = remote_of(wraps, half)
+        merged = wraps == 2
+        spans = spans_of(wraps, half)
+        origin = tok if merged else 0
+        if merged:
+            spans = spans[1:]
 
         def scores(i):
             at = pl.ds(pl.multiple_of(((group * steps + step) * STEP_HEADS + i) * HD, HD), HD)
             for first, last, keys in spans:
-                s_buf[i, first:last, : tiles(keys)] = jnp.dot(
-                    q_ref[first:last, at], xkt[group, :, : tiles(keys)],
+                s_buf[i % SLOTS, first:last, origin : tiles(keys)] = jnp.dot(
+                    q_ref[first:last, at], xkt[group, :, origin : tiles(keys)],
                     preferred_element_type=jnp.float32,
                 )
 
@@ -172,14 +175,18 @@
             head = (group * steps + step) * STEP_HEADS + i
             totals = {}
 
-            def add(j, part):
+            def add(at, part):
                 part = folded(part)
-                totals[j] = totals[j] + part if j in totals else part
+                totals[at] = totals[at] + part if at in totals else part
+
+            def clear(rows):
+                live = tiles(rows.stop)
+                if live < tok:
+                    w_ref[head, rows, live:tok] = jnp.zeros((CHUNK, tok - live), jnp.bfloat16)
 
             def merge_local(rows, scale, inverse):
                 inv_ref[head, rows] = inverse
-                live = tiles(rows.stop)
-                for at in range(0, live, LANES):
+                for at in range(0, tiles(rows.stop), LANES):
                     part = wl_ref[head, rows, at : at + LANES]
                     if scale is None:
                         w_ref[head, rows, at : at + LANES] = part
@@ -187,36 +194,48 @@
                     else:
                         part = part.astype(jnp.float32) * scale
                         w_ref[head, rows, at : at + LANES] = part.astype(jnp.bfloat16)
-                    add(at // LANES, part * inverse)
-                if live < tok:
-                    w_ref[head, rows, live:tok] = jnp.zeros((CHUNK, tok - live), jnp.bfloat16)
-
-            if wraps == 2:
+                    add(at, part * inverse)
+                clear(rows)
+
+            if merged:
                 for r in range(0, half, CHUNK):
                     rows = slice(r, r + CHUNK)
                     merge_local(rows, None, 1.0 / sum_ref[head, rows])
             for first, last, keys in spans:
                 for r in range(first, last, CHUNK):
                     rows = slice(r, r + CHUNK)
-                    parts = []
-                    for at in range(0, keys, LANES):
-                        part = s_buf[i, rows, at : at + LANES]
-                        parts.append(part + cut if at + LANES > keys else part)
-                    top = wide(jnp.max(functools.reduce(jnp.maximum, parts), axis=1, keepdims=True))
-                    top_l = top_ref[head, rows]
-                    top = jnp.maximum(top, top_l)
-                    scale = jnp.exp2((top_l - top) * EXP2_SCALE)
-                    parts = [jnp.exp2((part - top) * EXP2_SCALE) for part in parts]
-                    total = wide(jnp.sum(functools.reduce(jnp.add, parts), axis=1, keepdims=True))
-                    inverse = 1.0 / (sum_ref[head, rows] * scale + total)
-                    for j, part in enumerate(parts):
-                        w_ref[head, rows, tok + j * LANES : tok + (j + 1) * LANES] = part.astype(
-                            jnp.bfloat16
-                        )
-                        add(tok // LANES + j, part * inverse)
-                    merge_local(rows, scale, inverse)
-            for j, block in totals.items():
-                col[:, j * LANES : (j + 1) * LANES] += block
+                    parts = {}
+                    if not merged:
+                        for at in range(0, tiles(r + CHUNK), LANES):
+                            parts[at] = s_buf[i % SLOTS, rows, at : at + LANES]
+                            if at + LANES > r:
+                                parts[at] += bias[rows, at : at + LANES]
+                    for at in range(tok, keys, LANES):
+                        parts[at] = s_buf[i % SLOTS, rows, at : at + LANES]
+                        if at + LANES > keys:
+                            parts[at] += cut
+                    peak = functools.reduce(jnp.maximum, parts.values())
+                    top = wide(jnp.max(peak, axis=1, keepdims=True))
+                    if merged:
+                        top_l = top_ref[head, rows]
+                        top = jnp.maximum(top, top_l)
+                        scale = jnp.exp2((top_l - top) * EXP2_SCALE)
+                    parts = {at: jnp.exp2((part - top) * EXP2_SCALE) for at, part in parts.items()}
+                    total = functools.reduce(jnp.add, parts.values())
+                    total = wide(jnp.sum(total, axis=1, keepdims=True))
+                    if merged:
+                        total = sum_ref[head, rows] * scale + total
+                    inverse = 1.0 / total
+                    for at, part in parts.items():
+                        w_ref[head, rows, at : at + LANES] = part.astype(jnp.bfloat16)
+                        add(at, part * inverse)
+                    if merged:
+                        merge_local(rows, scale, inverse)
+                    else:
+                        inv_ref[head, rows] = inverse
+                        clear(rows)
+            for at, block in totals.items():
+                col[:, at : at + LANES] += block
 
         scores(0)
         for i in range(STEP_HEADS):
@@ -238,7 +257,6 @@
 
 def value_kernel(group, qpk, half, v_ref, v1_ref, v2_ref, w_ref, inv_ref, pass_ref, *refs):
     tok = 2 * half
-    steps = qpk // STEP_HEADS
     out_hbm, again_ref, xv, out_buf, sems = refs[-5:]
     again_ref[...] = pass_ref[...]
     at = slice(group * HD, (group + 1) * HD)
@@ -246,32 +264,30 @@
         [v_ref[:, at], v1_ref[:half, at], v2_ref[:half, at], v2_ref[half:, at], v1_ref[half:tok, at]], 0
     )
 
-    def sent(step):
-        first = (group * steps + step) * STEP_HEADS * HD
-        at = pl.ds(pl.multiple_of(first, HD), STEP_HEADS * HD)
-        return pltpu.make_async_copy(out_buf.at[step], out_hbm.at[:, at], sems.at[step])
-
-    def attend(wraps, step):
-        for i in range(STEP_HEADS):
-            lanes = slice(i * HD, (i + 1) * HD)
-            head = (group * steps + step) * STEP_HEADS + i
+    def sent(part):
+        first = (group * qpk + part * OUT_HEADS) * HD
+        at = slice(first, first + OUT_HEADS * HD)
+        return pltpu.make_async_copy(out_buf.at[part], out_hbm.at[:, at], sems.at[part])
+
+    @by_wraps
+    def _(wraps):
+        for i in range(qpk):
+            part, inside = divmod(i, OUT_HEADS)
+            lanes = slice(inside * HD, (inside + 1) * HD)
+            head = group * qpk + i
             for first, last, keys in spans_of(wraps, half):
                 product = jnp.dot(
                     w_ref[head, first:last, : tiles(keys)], xv[: tiles(keys)],
                     preferred_element_type=jnp.float32,
                 )
-                out_buf[step, first:last, lanes] = (product * inv_ref[head, first:last]).astype(
+                out_buf[part, first:last, lanes] = (product * inv_ref[head, first:last]).astype(
                     jnp.bfloat16
                 )
-        sent(step).start()
-
-    @by_wraps
-    def _(wraps):
-        pl.loop(0, steps)(functools.partial(attend, wraps))
-
-    @pl.loop(0, steps)
-    def _(step):
-        sent(step).wait()
+            if inside + 1 == OUT_HEADS:
+                sent(part).start()
+
+    for part in range(qpk // OUT_HEADS):
+        sent(part).wait()
 
 
 def cost(pairs, heads, half):
@@ -319,7 +335,7 @@
         scratch_shapes=[
             pltpu.VMEM((groups, HD, tok), jnp.bfloat16),
             pltpu.VMEM((tok, tok), jnp.float32),
-            pltpu.VMEM((STEP_HEADS, tok, tok), jnp.float32),
+            pltpu.VMEM((SLOTS, tok, tok), jnp.float32),
         ],
         compiler_params=pltpu.CompilerParams(vmem_limit_bytes=12 * MIB),
         cost_estimate=cost(3, heads, tok // 2),
@@ -327,7 +343,7 @@
     )(queries, keys)
 
 
-def remote_scores(queries, k2, k1, *local):
+def window_scores(queries, keys, k2, k1, *local):
     tok, width = queries.shape
     half = tok // 2
     groups = k1.shape[1] // HD
@@ -342,17 +358,18 @@
             line,
             line,
         ),
-        in_specs=[VMEM] * 6,
+        in_specs=[VMEM] * 7,
         out_specs=(VMEM,) * 5,
         scratch_shapes=[
-            pltpu.VMEM((groups, HD, 4 * half), jnp.bfloat16),
-            pltpu.VMEM((STEP_HEADS, tok, 4 * half), jnp.float32),
+            pltpu.VMEM((groups, HD, 6 * half), jnp.bfloat16),
+            pltpu.VMEM((tok, tok), jnp.float32),
+            pltpu.VMEM((SLOTS, tok, 6 * half), jnp.float32),
             pltpu.VMEM((8, 6 * half), jnp.float32),
         ],
-        compiler_params=pltpu.CompilerParams(vmem_limit_bytes=16 * MIB),
-        cost_estimate=cost(4, heads, half),
-        name="remote_scores",
-    )(queries, k2, k1, *local)
+        compiler_params=pltpu.CompilerParams(vmem_limit_bytes=20 * MIB),
+        cost_estimate=cost(7, heads, half),
+        name="window_scores",
+    )(queries, keys, k2, k1, *local)
 
 
 def ride(back, kept, v1):
@@ -393,7 +410,7 @@
 def window_values(group, values, v1, v2, weights, inverse, passed, *attended):
     heads, tok, most = weights.shape
     groups = values.shape[1] // HD
-    steps = heads // groups // STEP_HEADS
+    parts = heads // groups // OUT_HEADS
     return pl.pallas_call(
         functools.partial(value_kernel, group, heads // groups, tok // 2),
         out_shape=(
@@ -404,8 +421,8 @@
         out_specs=(HBM, VMEM),
         scratch_shapes=[
             pltpu.VMEM((most, HD), jnp.bfloat16),
-            pltpu.VMEM((steps, tok, STEP_HEADS * HD), jnp.bfloat16),
-            pltpu.SemaphoreType.DMA((steps,)),
+            pltpu.VMEM((parts, tok, OUT_HEADS * HD), jnp.bfloat16),
+            pltpu.SemaphoreType.DMA((parts,)),
         ],
         input_output_aliases={6: 0} if attended else {},
         compiler_params=pltpu.CompilerParams(vmem_limit_bytes=12 * MIB),
@@ -432,8 +449,8 @@
     )
     v1 = along(again1, 1)
     v2 = along(again2, 2)
-    weights, inverse, own, back1, back2 = remote_scores(
-        queries, k2, k1, *local_scores(queries, keys)
+    weights, inverse, own, back1, back2 = window_scores(
+        queries, keys, k2, k1, *local_scores(queries, keys)
     )
     tok = keys.shape[0]
     riding, stay = ride(back2, kept, v1)

time: 36.5 us -> 34.2 us (0.937); the launches traced: 36.3 us -> 33.5 us
  starting transfers between devices: 13.4 us -> 12.1 us
  Pallas kernels: 15.2 us -> 14 us
    ppermute x6, starting transfers between devices: 11.3 us -> 10.2 us  [along(): lax.ppermute(block, 'ctx', [(i, (i + distance) % count) for i in range(co...]
    ppermute x6, waiting for transfers between devices: 1.04 us -> 0.53 us  [along(): lax.ppermute(block, 'ctx', [(i, (i + distance) % count) for i in range(co...]
    pallas_call x2, Pallas kernels: 5.07 us -> 4.56 us  [window_values(): pl.pallas_call(functools.partial(value_kernel, group, heads // groups, to...]
    pallas_call x1, Pallas kernels: 3.03 us -> 2.62 us  [local_scores(): pl.pallas_call(functools.partial(local_kernel, groups, heads // groups, t...]
  transfers between devices with their start and end apart: 9 -> 9, of which waited for: 3 -> 2; matrix products, arithmetic and copies ran while one was open for 2% -> 2% of each run, Pallas kernels for 42% -> 42%
where the time goes in v3:
time: 34.2 us; the launch traced here: 33.5 us
  Pallas kernels  14 us (41%)
  starting transfers between devices  12.1 us (35%)
  local copies, waits for them, and re-layouts  4.56 us (13%)
  waiting for transfers between devices  1.3 us (4%)
  between operations  0.83 us (2%)
  other arithmetic  0.67 us (2%)
    ppermute x6, starting transfers between devices, along(): lax.ppermute(block, 'ctx', [(i, (i + distance) % count) for i in range(co...  10.2 us
    pallas_call x1, Pallas kernels, window_scores(): pl.pallas_call(functools.partial(score_kernel, groups, heads // groups, h...  5.48 us
    pallas_call x2, Pallas kernels, window_values(): pl.pallas_call(functools.partial(value_kernel, group, heads // groups, to...  4.56 us
    unnamed x16, local copies, waits for them, and re-layouts  3.91 us
    pallas_call x1, Pallas kernels, local_scores(): pl.pallas_call(functools.partial(local_kernel, groups, heads // groups, t...  2.62 us
    ppermute x3, starting transfers between devices, swap(): lax.ppermute(block, axis, [(i, i ^ bit) for i in range(lax.axis_size(axis...  1.93 us
    pallas_call x1, Pallas kernels, keep(): pl.pallas_call(functools.partial(keep_kernel, groups), out_shape=shapes,...  1.35 us
    ppermute x3, waiting for transfers between devices, swap(): lax.ppermute(block, axis, [(i, i ^ bit) for i in range(lax.axis_size(axis...  0.78 us
  transfers between devices with their start and end apart: 9, of which 2 were waited for; matrix products, arithmetic and copies ran while one was open for 2% of the time, Pallas kernels for 42%

profile of v3, /device:TPU:0, one launch (start us, length us, event | category | flops | bytes accessed | tf_op | source)
XLA Modules:
  0.0 33.5 jit_solution(16333165606703784746)
XLA Ops:
  0.6 3.1 %collective-permute-start.2 = (bf16[384,256]{1,0:T(8,128)(2,1)}, bf16[384,256]{1,0:T(8,128)(2,1)S(1)}, u32[]{:S(2)}, u32[]{:S(2)}) collective-permute-start(bf16[384,256]{1,0:T(8,128)(2,1)} %k_ref.5), channel_id=1, source_target_pairs={{0,8},{4,12},{8,16},{12,20},{16,24},{20,28},{24,0},{28,4},{1,9},{5... | collective-permute-start | bytes 589832 | tf_op jit(solution)/shard_map/ppermute | solution.py:440
  3.7 1.5 %collective-permute-start.3 = (bf16[384,256]{1,0:T(8,128)(2,1)}, bf16[384,256]{1,0:T(8,128)(2,1)S(1)}, u32[]{:S(2)}, u32[]{:S(2)}) collective-permute-start(bf16[384,256]{1,0:T(8,128)(2,1)} %k_ref.5), channel_id=1, source_target_pairs={{0,4},{4,8},{8,12},{12,16},{16,20},{20,24},{24,28},{28,0},{1,5},{5... | collective-permute-start | bytes 589832 | tf_op jit(solution)/shard_map/ppermute | solution.py:440
  5.2 0.9 %copy-done = bf16[384,256]{1,0:T(8,128)(2,1)S(1)} copy-done((bf16[384,256]{1,0:T(8,128)(2,1)S(1)}, bf16[384,256]{1,0:T(8,128)(2,1)}, u32[]{:S(2)}) %copy-start) | copy-done | bytes 196632
  6.1 0.9 %copy-done.3 = bf16[384,256]{1,0:T(8,128)(2,1)S(1)} copy-done((bf16[384,256]{1,0:T(8,128)(2,1)S(1)}, bf16[384,256]{1,0:T(8,128)(2,1)}, u32[]{:S(2)}) %copy-start.3) | copy-done | bytes 196632
  7.1 0.7 %copy-done.5 = s32[1,2,8,4]{2,3,1,0:T(4,128)S(1)} copy-done((s32[1,2,8,4]{2,3,1,0:T(4,128)S(1)}, s32[1,2,8,4]{2,3,1,0:T(4,128)}, u32[]{:S(2)}) %copy-start.5) | copy-done | bytes 280
  7.7 0.7 %copy-done.6 = s32[1,2,8]{2,1,0:T(2,128)S(1)} copy-done((s32[1,2,8]{2,1,0:T(2,128)S(1)}, s32[1,2,8]{2,1,0:T(2,128)}, u32[]{:S(2)}) %copy-start.6) | copy-done | bytes 88
  8.4 0.7 %copy-done.7 = s32[1,2,8]{2,1,0:T(2,128)S(1)} copy-done((s32[1,2,8]{2,1,0:T(2,128)S(1)}, s32[1,2,8]{2,1,0:T(2,128)}, u32[]{:S(2)}) %copy-start.7) | copy-done | bytes 88
  9.1 1.3 %keep_rows.1 = (bf16[32,256]{1,0:T(8,128)(2,1)S(1)}, bf16[416,256]{1,0:T(8,128)(2,1)S(1)}, bf16[384,256]{1,0:T(8,128)(2,1)S(1)}, s32[8,256]{1,0:T(8,128)S(1)}, s...) custom-call(bf16[384,256]{1,0:T(8,128)(2,1)S(1)} %copy-done.3, bf16[384,256]{1,0:T(8,128)(2,1)S(1)} %copy-done, ...), custom_call_target="tpu_custom_call" | custom-call | flops 1811939328 | bytes 25165824 | tf_op jit(solution)/shard_map/keep_rows/pallas_call | solution.py:312
  10.5 1.6 %collective-permute-start = (bf16[416,256]{1,0:T(8,128)(2,1)S(1)}, bf16[416,256]{1,0:T(8,128)(2,1)S(1)}, u32[]{:S(2)}, u32[]{:S(2)}) collective-permute-start(bf16[416,256]{1,0:T(8,128)(2,1)S(1)} %get-tuple-element.23), channel_id=1, source_target_pairs={{0,4},{4,8},{8,12},{12,16},{16,20},{20,24},{24,28},{28,0},{1,5},{5... | collective-permute-start | bytes 638984 | tf_op jit(solution)/shard_map/ppermute | solution.py:440
  12.1 1.6 %collective-permute-start.1 = (bf16[384,256]{1,0:T(8,128)(2,1)S(1)}, bf16[384,256]{1,0:T(8,128)(2,1)S(1)}, u32[]{:S(2)}, u32[]{:S(2)}) collective-permute-start(bf16[384,256]{1,0:T(8,128)(2,1)S(1)} %get-tuple-element.24), channel_id=1, source_target_pairs={{0,8},{4,12},{8,16},{12,20},{16,24},{20,28},{24,0},{28,4},{1,9},{5... | collective-permute-start | bytes 589832 | tf_op jit(solution)/shard_map/ppermute | solution.py:440
  13.6 0.0 copy-done.2
  13.6 0.0 copy-done.4
  13.6 2.6 %local_scores.1 = (bf16[16,384,384]{2,1,0:T(8,128)(2,1)S(1)}, f32[16,384,128]{2,1,0:T(8,128)S(1)}, f32[16,384,128]{2,1,0:T(8,128)S(1)}) custom-call(bf16[384,2048]{1,0:T(8,128)(2,1)S(1)} %copy-done.2, bf16[384,256]{1,0:T(8,128)(2,1)S(1)} %copy-done.4), custom_call_target="tpu_custom_call" | custom-call | flops 2717908992 | bytes 25165824 | tf_op jit(solution)/shard_map/local_scores/pallas_call | solution.py:330
  16.3 0.0 collective-permute-done.2.k2_ref
  16.3 0.5 %collective-permute-done.3.k1_ref = bf16[384,256]{1,0:T(8,128)(2,1)S(1)} collective-permute-done((bf16[384,256]{1,0:T(8,128)(2,1)}, bf16[384,256]{1,0:T(8,128)(2,1)S(1)}, u32[]{:S(2)}, u32[]{:S(2)}) %collective-permute-start.3) | collective-permute-done | bytes 196640 | tf_op jit(solution)/shard_map/ppermute | solution.py:440
  16.8 5.5 %window_scores.1 = (bf16[16,384,1152]{2,1,0:T(8,128)(2,1)S(1)}, f32[16,384,128]{2,1,0:T(8,128)S(1)}, f32[1,384]{1,0:T(1,128)S(1)}, f32[1,384]{1,0:T(1,128)S(1)}, f32[1,384]{1,0:T(1,128)S(1)}) custom-call(bf16[384,2048]{1,0:T(8,128)(2,1)S(1)} %copy-done.2, bf16[384,256]{1,0:T(8,128)(2,1)S(1)} %copy-done.4, ...), custom_call_target="tpu_custom_call" | custom-call | flops 6341787648 | bytes 25165824 | tf_op jit(solution)/shard_map/window_scores/pallas_call | solution.py:352
  22.3 0.4 %collective-permute-start.4 = (f32[1,384]{1,0:T(1,128)S(1)}, f32[1,384]{1,0:T(1,128)S(1)}, u32[]{:S(2)}, u32[]{:S(2)}) collective-permute-start(f32[1,384]{1,0:T(1,128)S(1)} %get-tuple-element.32), channel_id=1, source_target_pairs={{0,28},{4,0},{8,4},{12,8},{16,12},{20,16},{24,20},{28,24},{1,29},{... | collective-permute-start | bytes 4616 | tf_op jit(solution)/shard_map/ppermute | solution.py:440
  22.7 0.0 collective-permute-done.v1_ref
  22.7 2.1 %collective-permute-start.5 = (f32[40,256]{1,0:T(8,128)S(1)}, f32[40,256]{1,0:T(8,128)S(1)}, u32[]{:S(2)}, u32[]{:S(2)}) collective-permute-start(f32[40,256]{1,0:T(8,128)S(1)} %get-tuple-element.35), channel_id=1, source_target_pairs={{0,24},{4,28},{8,0},{12,4},{16,8},{20,12},{24,16},{28,20},{1,25},{... | collective-permute-start | bytes 122888 | tf_op jit(solution)/shard_map/ppermute | solution.py:440
  24.8 0.0 collective-permute-done.1.v2_ref
  24.8 2.4 %window_values.2 = (bf16[384,2048]{1,0:T(8,128)(2,1)}, f32[1,384]{1,0:T(1,128)S(1)}) custom-call(bf16[384,256]{1,0:T(8,128)(2,1)S(1)} %copy-done.1, bf16[416,256]{1,0:T(8,128)(2,1)S(1)} %collective-permute-done.v1_ref, bf16[384,256]{1,0:T(8,128)(2,1)S(1)} %collective-permute-done.1.v2_ref, bf16[16,384,1152]{2,1,0:T(8,128)(2,1)S(1)} %get-tuple-element.28.w_ref, ...), custom_call_target="tpu_custom_call" | custom-call | flops 1358954496 | bytes 12582912 | tf_op jit(solution)/shard_map/window_values/pallas_call | solution.py:414
  27.2 0.0 collective-permute-done.5
  27.2 0.0 collective-permute-done.4
  27.2 0.1 collective-permute-start.6
  27.4 0.3 %collective-permute-start.8 = (bf16[1,2,2,1,8,256]{5,4,3,2,1,0:T(8,128)(2,1)S(1)}, bf16[1,2,2,1,8,256]{5,4,3,2,1,0:T(8,128)(2,1)S(1)}, u32[]{:S(2)}, u32[]{:S(2)}) collective-permute-start(bf16[1,2,2,1,8,256]{5,4,3,2,1,0:T(8,128)(2,1)S(1)} %broadcast_select_fusion.3), channel_id=1, source_target_pairs={{0,16},{4,20},{8,24},{12,28},{16,0},{20,4},{24,8},{28,12},{1,17},{... | collective-permute-start | bytes 49160 | tf_op jit(solution)/shard_map/ppermute | solution.py:443
  27.7 0.8 %collective-permute-done.6 = f32[1,384]{1,0:T(1,128)S(1)} collective-permute-done((f32[1,384]{1,0:T(1,128)S(1)}, f32[1,384]{1,0:T(1,128)S(1)}, u32[]{:S(2)}, u32[]{:S(2)}) %collective-permute-start.6) | collective-permute-done | bytes 1568 | tf_op jit(solution)/shard_map/ppermute | solution.py:443
  28.5 1.5 %collective-permute-start.7 = (f32[1,384]{1,0:T(1,128)S(1)}, f32[1,384]{1,0:T(1,128)S(1)}, u32[]{:S(2)}, u32[]{:S(2)}) collective-permute-start(f32[1,384]{1,0:T(1,128)S(1)} %add.14.pass_ref), channel_id=1, source_target_pairs={{0,2},{1,3},{2,0},{3,1},{4,6},{5,7},{6,4},{7,5},{8,10},{9,11},{10,... | collective-permute-start | bytes 4616 | tf_op jit(solution)/shard_map/ppermute | solution.py:443
  30.0 2.2 %window_values.3 = (bf16[384,2048]{1,0:T(8,128)(2,1)}, f32[1,384]{1,0:T(1,128)S(1)}) custom-call(bf16[384,256]{1,0:T(8,128)(2,1)S(1)} %copy-done.1, bf16[416,256]{1,0:T(8,128)(2,1)S(1)} %collective-permute-done.v1_ref, bf16[384,256]{1,0:T(8,128)(2,1)S(1)} %collective-permute-done.1.v2_ref, ...), custom_call_target="tpu_custom_call", output_to_operand_aliasing={{0}: (6, {})} | custom-call | flops 1358954496 | bytes 12582912 | tf_op jit(solution)/shard_map/window_values/pallas_call | solution.py:414
  32.2 0.0 collective-permute-done.7
  32.2 0.6 %add_reduce_fusion = f32[384]{0:T(512)} fusion(f32[1,384]{1,0:T(1,128)S(1)} %get-tuple-element.38, f32[1,384]{1,0:T(1,128)S(1)} %collective-permute-done.7), kind=kLoop, calls=%fused_computation.21 | loop fusion | flops 384 | bytes 4608 | tf_op jit(solution)/shard_map/add | solution.py:484
  32.8 0.0 collective-permute-done.8
  32.9 0.6 %reshape_reshape.3 = bf16[1,8,4,2,256]{4,3,2,1,0:T(2,128)(2,1)} reshape(bf16[4,2,8,256]{3,2,1,0:T(8,128)(2,1)S(1)} %pad_maximum_fusion.1) | data formatting | bytes 65536 | tf_op jit(solution)/shard_map/reshape;reshape | solution.py:499
  (26 shorter events, 0.1 us)
Async XLA Ops:
  0.6 15.7 %collective-permute-start.2 = (bf16[384,256]{1,0:T(8,128)(2,1)}, bf16[384,256]{1,0:T(8,128)(2,1)S(1)}, u32[]{:S(2)}, u32[]{:S(2)}) collective-permute-start(bf16[384,256]{1,0:T(8,128)(2,1)} %k_ref.5), channel_id=1, source_target_pairs={{0,8},{4,12},{8,16},{12,20},{16,24},{20,28},{24,0},{28,4},{1,9},{5... | collective-permute-start | bytes 589832 | tf_op jit(solution)/shard_map/ppermute | solution.py:440
  3.7 13.1 %collective-permute-start.3 = (bf16[384,256]{1,0:T(8,128)(2,1)}, bf16[384,256]{1,0:T(8,128)(2,1)S(1)}, u32[]{:S(2)}, u32[]{:S(2)}) collective-permute-start(bf16[384,256]{1,0:T(8,128)(2,1)} %k_ref.5), channel_id=1, source_target_pairs={{0,4},{4,8},{8,12},{12,16},{16,20},{20,24},{24,28},{28,0},{1,5},{5... | collective-permute-start | bytes 589832 | tf_op jit(solution)/shard_map/ppermute | solution.py:440
  5.2 0.9 %copy-start = (bf16[384,256]{1,0:T(8,128)(2,1)S(1)}, bf16[384,256]{1,0:T(8,128)(2,1)}, u32[]{:S(2)}) copy-start(bf16[384,256]{1,0:T(8,128)(2,1)} %v_ref.5) | copy-start | bytes 589828
  6.1 0.9 %copy-start.3 = (bf16[384,256]{1,0:T(8,128)(2,1)S(1)}, bf16[384,256]{1,0:T(8,128)(2,1)}, u32[]{:S(2)}) copy-start(bf16[384,256]{1,0:T(8,128)(2,1)} %k_ref.5) | copy-start | bytes 589828
  7.1 0.7 %copy-start.5 = (s32[1,2,8,4]{2,3,1,0:T(4,128)S(1)}, s32[1,2,8,4]{2,3,1,0:T(4,128)}, u32[]{:S(2)}) copy-start(s32[1,2,8,4]{2,3,1,0:T(4,128)} %param.9) | copy-start | bytes 772
  7.7 0.7 %copy-start.6 = (s32[1,2,8]{2,1,0:T(2,128)S(1)}, s32[1,2,8]{2,1,0:T(2,128)}, u32[]{:S(2)}) copy-start(s32[1,2,8]{2,1,0:T(2,128)} %dest_hbm.1) | copy-start | bytes 196
  8.4 0.7 %copy-start.7 = (s32[1,2,8]{2,1,0:T(2,128)S(1)}, s32[1,2,8]{2,1,0:T(2,128)}, u32[]{:S(2)}) copy-start(s32[1,2,8]{2,1,0:T(2,128)} %live_hbm.1) | copy-start | bytes 196
  9.1 4.5 %copy-start.2 = (bf16[384,2048]{1,0:T(8,128)(2,1)S(1)}, bf16[384,2048]{1,0:T(8,128)(2,1)}, u32[]{:S(2)}) copy-start(bf16[384,2048]{1,0:T(8,128)(2,1)} %q_ref.3) | copy-start | bytes 4718596
  9.1 4.5 %copy-start.4 = (bf16[384,256]{1,0:T(8,128)(2,1)S(1)}, bf16[384,256]{1,0:T(8,128)(2,1)}, u32[]{:S(2)}) copy-start(bf16[384,256]{1,0:T(8,128)(2,1)} %k_ref.5) | copy-start | bytes 589828
  10.5 12.2 %collective-permute-start = (bf16[416,256]{1,0:T(8,128)(2,1)S(1)}, bf16[416,256]{1,0:T(8,128)(2,1)S(1)}, u32[]{:S(2)}, u32[]{:S(2)}) collective-permute-start(bf16[416,256]{1,0:T(8,128)(2,1)S(1)} %get-tuple-element.23), channel_id=1, source_target_pairs={{0,4},{4,8},{8,12},{12,16},{16,20},{20,24},{24,28},{28,0},{1,5},{5... | collective-permute-start | bytes 638984 | tf_op jit(solution)/shard_map/ppermute | solution.py:440
  12.1 12.7 %collective-permute-start.1 = (bf16[384,256]{1,0:T(8,128)(2,1)S(1)}, bf16[384,256]{1,0:T(8,128)(2,1)S(1)}, u32[]{:S(2)}, u32[]{:S(2)}) collective-permute-start(bf16[384,256]{1,0:T(8,128)(2,1)S(1)} %get-tuple-element.24), channel_id=1, source_target_pairs={{0,8},{4,12},{8,16},{12,20},{16,24},{20,28},{24,0},{28,4},{1,9},{5... | collective-permute-start | bytes 589832 | tf_op jit(solution)/shard_map/ppermute | solution.py:440
  16.8 8.0 %copy-start.1 = (bf16[384,256]{1,0:T(8,128)(2,1)S(1)}, bf16[384,256]{1,0:T(8,128)(2,1)}, u32[]{:S(2)}) copy-start(bf16[384,256]{1,0:T(8,128)(2,1)} %v_ref.5) | copy-start | bytes 589828
  22.3 4.9 %collective-permute-start.4 = (f32[1,384]{1,0:T(1,128)S(1)}, f32[1,384]{1,0:T(1,128)S(1)}, u32[]{:S(2)}, u32[]{:S(2)}) collective-permute-start(f32[1,384]{1,0:T(1,128)S(1)} %get-tuple-element.32), channel_id=1, source_target_pairs={{0,28},{4,0},{8,4},{12,8},{16,12},{20,16},{24,20},{28,24},{1,29},{... | collective-permute-start | bytes 4616 | tf_op jit(solution)/shard_map/ppermute | solution.py:440
  22.7 4.5 %collective-permute-start.5 = (f32[40,256]{1,0:T(8,128)S(1)}, f32[40,256]{1,0:T(8,128)S(1)}, u32[]{:S(2)}, u32[]{:S(2)}) collective-permute-start(f32[40,256]{1,0:T(8,128)S(1)} %get-tuple-element.35), channel_id=1, source_target_pairs={{0,24},{4,28},{8,0},{12,4},{16,8},{20,12},{24,16},{28,20},{1,25},{... | collective-permute-start | bytes 122888 | tf_op jit(solution)/shard_map/ppermute | solution.py:440
  27.2 1.2 %collective-permute-start.6 = (f32[1,384]{1,0:T(1,128)S(1)}, f32[1,384]{1,0:T(1,128)S(1)}, u32[]{:S(2)}, u32[]{:S(2)}) collective-permute-start(f32[1,384]{1,0:T(1,128)S(1)} %fusion.1), channel_id=1, source_target_pairs={{0,1},{1,0},{2,3},{3,2},{4,5},{5,4},{6,7},{7,6},{8,9},{9,8},{10,11... | collective-permute-start | bytes 4616 | tf_op jit(solution)/shard_map/ppermute | solution.py:443
  27.4 5.4 %collective-permute-start.8 = (bf16[1,2,2,1,8,256]{5,4,3,2,1,0:T(8,128)(2,1)S(1)}, bf16[1,2,2,1,8,256]{5,4,3,2,1,0:T(8,128)(2,1)S(1)}, u32[]{:S(2)}, u32[]{:S(2)}) collective-permute-start(bf16[1,2,2,1,8,256]{5,4,3,2,1,0:T(8,128)(2,1)S(1)} %broadcast_select_fusion.3), channel_id=1, source_target_pairs={{0,16},{4,20},{8,24},{12,28},{16,0},{20,4},{24,8},{28,12},{1,17},{... | collective-permute-start | bytes 49160 | tf_op jit(solution)/shard_map/ppermute | solution.py:443
  28.5 3.7 %collective-permute-start.7 = (f32[1,384]{1,0:T(1,128)S(1)}, f32[1,384]{1,0:T(1,128)S(1)}, u32[]{:S(2)}, u32[]{:S(2)}) collective-permute-start(f32[1,384]{1,0:T(1,128)S(1)} %add.14.pass_ref), channel_id=1, source_target_pairs={{0,2},{1,3},{2,0},{3,1},{4,6},{5,7},{6,4},{7,5},{8,10},{9,11},{10,... | collective-permute-start | bytes 4616 | tf_op jit(solution)/shard_map/ppermute | solution.py:443
